TPU v7x, 32 devices: a whole 2x2x4 slice. The times are simulated.
32 devices in a mesh: gx: 2 (over x), gy: 4 (over y, core), gz: 4 (over z).
Axes of the slice: x: 2, y: 2, z: 4, core: 2. Of those that a mesh axis runs over, the one named last changes fastest.
Arguments:
- node_feats: bfloat16 [64, 16384], P(None, ('gx', 'gy', 'gz')), may hold values from -6 to 6
- edge_vectors: float32 [3, 65536], P(None, ('gx', 'gy', 'gz')), may hold values from -4.95 to 4.95, as said below
- edge_source: int32 [65536], P(('gx', 'gy', 'gz')), may hold values from 0 to 1279
- edge_target: int32 [65536], P(('gx', 'gy', 'gz')), may hold values from 0 to 511
- edge_count: int32 [32], P(('gx', 'gy', 'gz')), may hold values from 1 to 2048, 40960 in all
- halo_index: int32 [6, 4096], P(None, ('gx', 'gy', 'gz')), may hold values from 0 to 511
- atom_species: int32 [16384], P(('gx', 'gy', 'gz')), may hold values from 0 to 3
- site_cotangent: float32 [16384], P(('gx', 'gy', 'gz')), may hold values from -6 to 6
- radial_input: float32 [8, 64], replicated, may hold values from -12 to 12
- radial_hidden: float32 [2, 64, 64], replicated, may hold values from -1.2 to 1.2
- radial_output: float32 [64, 256], replicated, may hold values from -0.75 to 0.75
- degree_mix: float32 [4, 64, 64], replicated, may hold values from -0.75 to 0.75
- species_mix: float32 [4, 64, 64], replicated, may hold values from -0.75 to 0.75
- readout_weights: float32 [2, 64], replicated, may hold values from -0.75 to 0.75
- moment_radial_input: float32 [8, 64], replicated, may hold values from -6 to 6
- moment_radial_hidden: float32 [2, 64, 64], replicated, may hold values from -6 to 6
- moment_radial_output: float32 [64, 256], replicated, may hold values from -6 to 6
- moment_degree_mix: float32 [4, 64, 64], replicated, may hold values from -6 to 6
- moment_species_mix: float32 [4, 64, 64], replicated, may hold values from -6 to 6
- moment_readout_weights: float32 [2, 64], replicated, may hold values from -40 to 40
- square_radial_input: float32 [8, 64], replicated, may hold values from 0.16384 to 0.65536
- square_radial_hidden: float32 [2, 64, 64], replicated, may hold values from 0.16384 to 0.65536
- square_radial_output: float32 [64, 256], replicated, may hold values from 0.16384 to 0.65536
- square_degree_mix: float32 [4, 64, 64], replicated, may hold values from 0.16384 to 0.65536
- square_species_mix: float32 [4, 64, 64], replicated, may hold values from 0.16384 to 0.65536
- square_readout_weights: float32 [2, 64], replicated, may hold values from 4.096 to 16.384
Outputs:
- site_energy: float32 [16384], P(('gx', 'gy', 'gz'))
- feature_grad: float32 [64, 16384], P(None, ('gx', 'gy', 'gz'))
- position_grad: float32 [3, 16384], P(None, ('gx', 'gy', 'gz'))
- updated_radial_input: float32 [8, 64], replicated
- updated_radial_hidden: float32 [2, 64, 64], replicated
- updated_radial_output: float32 [64, 256], replicated
- updated_degree_mix: float32 [4, 64, 64], replicated
- updated_species_mix: float32 [4, 64, 64], replicated
- updated_readout_weights: float32 [2, 64], replicated
- updated_moment_radial_input: float32 [8, 64], replicated
- updated_moment_radial_hidden: float32 [2, 64, 64], replicated
- updated_moment_radial_output: float32 [64, 256], replicated
- updated_moment_degree_mix: float32 [4, 64, 64], replicated
- updated_moment_species_mix: float32 [4, 64, 64], replicated
- updated_moment_readout_weights: float32 [2, 64], replicated
- updated_square_radial_input: float32 [8, 64], replicated
- updated_square_radial_hidden: float32 [2, 64, 64], replicated
- updated_square_radial_output: float32 [64, 256], replicated
- updated_square_degree_mix: float32 [4, 64, 64], replicated
- updated_square_species_mix: float32 [4, 64, 64], replicated
- updated_square_readout_weights: float32 [2, 64], replicated
Inputs may be any that keep to these rules, and one draw needn't show every extreme that they name: `edge_source`: indices into the device's extended list: its own 512 atoms, then 128 atoms from the lower and from the upper neighbour along gx, gy, gz in that order. `edge_target`: local atom of the same device. `edge_count`: slots at this position of the device's list or later are unused; some device uses all 2048. `halo_index`: row 2k lists local atoms that the upper neighbour along the k-th axis reads, row 2k + 1 those that the lower one reads; repeats are allowed. `edge_vectors`: every column has a length between 0.8 and 4.95.
All inputs are finite; a program needn't handle non-finite values.
Results may differ from a plain program's by a relative error of at most 0.004.
The roundings to bfloat16 on the way count: a program that leaves them out, or rounds other values in their place, can miss the bound.
Values may be sent and summed in bfloat16 or wider, within the bound.
No kernel may reach another device: no remote copies, remote signals or barrier semaphores. Data moves between devices by JAX's collectives and lax.ppermute only.
A program may use at most 128 MiB of HBM per device.

v0:
```python
import math

import jax
import jax.numpy as jnp
from jax import lax
from jax.sharding import PartitionSpec as P

NBASIS = 8
STEP = 10


CUTOFF = 5.0
BESSEL_NORM = math.sqrt(2.0 / 5.0)
SQRT3 = math.sqrt(3.0)
SQRT5 = math.sqrt(5.0)
SQRT7 = math.sqrt(7.0)
SQRT15 = math.sqrt(15.0)
CUBIC_A = math.sqrt(35.0 / 8.0)
CUBIC_B = math.sqrt(105.0)
CUBIC_C = math.sqrt(21.0 / 8.0)
BETA_ONE = 0.9
BETA_TWO = 0.999
EPSILON = 1e-08
DECAY = 0.01
RATES = (2.0, 0.2, 0.125, 0.125, 0.125, 0.125)
DEGREE_SLICES = ((0, 1), (1, 4), (4, 9), (9, 16))


def shifted(value, axis, steps):
    count = lax.axis_size(axis)
    pairs = [(source, (source + steps) % count) for source in range(count)]
    return lax.ppermute(value, axis, pairs)


def harmonics(direction):
    along_x, along_y, along_z = (direction[0], direction[1], direction[2])
    square_z = along_z * along_z
    return jnp.stack(
        [
            jnp.ones_like(along_x),
            SQRT3 * along_x,
            SQRT3 * along_y,
            SQRT3 * along_z,
            SQRT15 * along_x * along_y,
            SQRT15 * along_y * along_z,
            0.5 * SQRT5 * (3.0 * square_z - 1.0),
            SQRT15 * along_x * along_z,
            0.5 * SQRT15 * (along_x * along_x - along_y * along_y),
            CUBIC_A * along_y * (3.0 * along_x * along_x - along_y * along_y),
            CUBIC_B * along_x * along_y * along_z,
            CUBIC_C * along_y * (5.0 * square_z - 1.0),
            0.5 * SQRT7 * along_z * (5.0 * square_z - 3.0),
            CUBIC_C * along_x * (5.0 * square_z - 1.0),
            0.5 * CUBIC_B * along_z * (along_x * along_x - along_y * along_y),
            CUBIC_A * along_x * (along_x * along_x - 3.0 * along_y * along_y),
        ]
    )


def geometry(relative):
    distance = jnp.sqrt(jnp.sum(relative * relative, axis=0))
    scaled_dist = distance / CUTOFF
    power_six = scaled_dist**6
    envelope = (
        1.0
        - 28.0 * power_six
        + 48.0 * power_six * scaled_dist
        - 21.0 * power_six * scaled_dist * scaled_dist
    )
    orders = jnp.arange(1, NBASIS + 1).astype(relative.dtype)[:, None]
    bessel = (
        BESSEL_NORM
        * jnp.sin(orders * (math.pi / CUTOFF) * distance[None, :])
        / distance[None, :]
        * envelope[None, :]
    )
    return (bessel, harmonics(relative / distance[None, :]))


def silu_slope(values):
    logistic = jax.nn.sigmoid(values)
    return logistic * (1.0 + values * (1.0 - logistic))


def adamw_update(weight, moment, square, gradient, step_rate):
    moment = BETA_ONE * moment + (1.0 - BETA_ONE) * gradient
    square = BETA_TWO * square + (1.0 - BETA_TWO) * gradient * gradient
    corrected = (
        moment / (1.0 - BETA_ONE**STEP) / (jnp.sqrt(square / (1.0 - BETA_TWO**STEP)) + EPSILON)
    )
    return (weight - step_rate * (corrected + DECAY * weight), moment, square)


def forward_face(outgoing, axis_pos, direction):
    if axis_pos == 0:
        return shifted(outgoing, "gx", direction)
    if axis_pos == 1:
        return shifted(outgoing, "gy", direction)
    return shifted(outgoing, "gz", direction)


def backward_face(outgoing, axis_pos, direction):
    if axis_pos == 0:
        return shifted(outgoing, "gx", direction)
    if axis_pos == 1:
        return shifted(outgoing, "gy", direction)
    return shifted(outgoing, "gz", direction)


def project(weight, values):
    return jnp.einsum("fk,fe->ke", weight, values, preferred_element_type=jnp.float32)


def project_back(weight, values):
    return jnp.einsum("fk,ke->fe", weight, values, preferred_element_type=jnp.float32)


def outer_sum(left, right):
    return jnp.einsum("fe,ke->fk", left, right, preferred_element_type=jnp.float32)


def on_device(
    node_feats,
    edge_vectors,
    edge_source,
    edge_target,
    edge_count,
    halo_index,
    atom_species,
    site_cotangent,
    radial_input,
    radial_hidden,
    radial_output,
    degree_mix,
    species_mix,
    readout_weights,
    moment_radial_input,
    moment_radial_hidden,
    moment_radial_output,
    moment_degree_mix,
    moment_species_mix,
    moment_readout_weights,
    square_radial_input,
    square_radial_hidden,
    square_radial_output,
    square_degree_mix,
    square_species_mix,
    square_readout_weights,
):
    masters = (radial_input, radial_hidden, radial_output, degree_mix, species_mix, readout_weights)
    moments = (
        moment_radial_input,
        moment_radial_hidden,
        moment_radial_output,
        moment_degree_mix,
        moment_species_mix,
        moment_readout_weights,
    )
    squares = (
        square_radial_input,
        square_radial_hidden,
        square_radial_output,
        square_degree_mix,
        square_species_mix,
        square_readout_weights,
    )
    channels, local_atoms = node_feats.shape
    halo_width = halo_index.shape[1]
    slot_count = edge_vectors.shape[1]
    inverse_avg = 1.0 / max(1, 5 * slot_count // (8 * local_atoms))
    w_in, w_hidden, w_out, w_degree, w_species = [
        weight.astype(jnp.bfloat16) for weight in masters[:5]
    ]
    pieces = [node_feats]
    for axis_pos in range(3):
        for direction in (1, -1):
            face_row = 2 * axis_pos + (0 if direction == 1 else 1)
            outgoing = jnp.take(node_feats, halo_index[face_row], axis=1)
            pieces.append(forward_face(outgoing, axis_pos, direction))
    extended = jnp.concatenate(pieces, axis=1)
    bessel, harmonic = geometry(edge_vectors)
    live_mask = (lax.iota(jnp.int32, slot_count) < edge_count[0]).astype(jnp.float32)
    bessel_low = bessel.astype(jnp.bfloat16)
    pre_one = project(w_in, bessel_low)
    act_one = jax.nn.silu(pre_one).astype(jnp.bfloat16)
    pre_two = project(w_hidden[0], act_one)
    act_two = jax.nn.silu(pre_two).astype(jnp.bfloat16)
    pre_three = project(w_hidden[1], act_two)
    act_three = jax.nn.silu(pre_three).astype(jnp.bfloat16)
    radial = project(w_out, act_three).reshape(4, channels, slot_count)
    weighted = jnp.take(extended, edge_source, axis=1).astype(jnp.float32) * live_mask[None, :]
    spread = jnp.concatenate(
        [
            jnp.broadcast_to(radial[degree][None], (last - first, channels, slot_count))
            for degree, (first, last) in enumerate(DEGREE_SLICES)
        ],
        axis=0,
    )
    message = spread * harmonic[:, None, :] * weighted[None]
    summed = (
        jnp.zeros((16, channels, local_atoms), jnp.float32).at[:, :, edge_target].add(message)
        * inverse_avg
    )
    summed_low = summed.astype(jnp.bfloat16)
    mixed = jnp.concatenate(
        [
            jnp.einsum(
                "cd,kci->kdi",
                w_degree[degree],
                summed_low[first:last],
                preferred_element_type=jnp.float32,
            )
            for degree, (first, last) in enumerate(DEGREE_SLICES)
        ],
        axis=0,
    )
    species_mask = (
        atom_species[None, :] == lax.iota(jnp.int32, w_species.shape[0])[:, None]
    ).astype(jnp.float32)
    per_species = jnp.einsum(
        "zcd,ci->zdi", w_species, node_feats, preferred_element_type=jnp.float32
    )
    self_term = jnp.sum(per_species * species_mask[:, None, :], axis=0)
    scalars = mixed[0] + self_term
    gate = jax.nn.sigmoid(scalars)
    scalar_out = scalars * gate
    gated = mixed[1:] * gate[None]
    quadratic = jnp.sum(gated * gated, axis=0)
    site_energy = jnp.sum(
        readout_weights[0][:, None] * scalar_out + readout_weights[1][:, None] * quadratic, axis=0
    )
    grad_readout = jnp.stack(
        [
            jnp.sum(scalar_out * site_cotangent[None, :], axis=1),
            jnp.sum(quadratic * site_cotangent[None, :], axis=1),
        ]
    )
    back_out = readout_weights[0][:, None] * site_cotangent[None, :]
    back_quad = readout_weights[1][:, None] * site_cotangent[None, :]
    back_gated = 2.0 * gated * back_quad[None]
    back_gate = jnp.sum(back_gated * mixed[1:], axis=0)
    back_scalars = back_out * silu_slope(scalars) + back_gate * gate * (1.0 - gate)
    back_mixed = jnp.concatenate([back_scalars[None], back_gated * gate[None]], axis=0).astype(
        jnp.bfloat16
    )
    back_self = back_scalars.astype(jnp.bfloat16)
    grad_degree = jnp.stack(
        [
            jnp.einsum(
                "kci,kdi->cd",
                summed_low[first:last],
                back_mixed[first:last],
                preferred_element_type=jnp.float32,
            )
            for first, last in DEGREE_SLICES
        ]
    )
    back_summed = jnp.concatenate(
        [
            jnp.einsum(
                "cd,kdi->kci",
                w_degree[degree],
                back_mixed[first:last],
                preferred_element_type=jnp.float32,
            )
            for degree, (first, last) in enumerate(DEGREE_SLICES)
        ],
        axis=0,
    )
    mask_low = species_mask.astype(jnp.bfloat16)
    grad_species = jnp.einsum(
        "zci,di->zcd",
        node_feats[None] * mask_low[:, None, :],
        back_self,
        preferred_element_type=jnp.float32,
    )
    back_local = jnp.einsum(
        "zcd,zdi->ci",
        w_species,
        mask_low[:, None, :] * back_self[None],
        preferred_element_type=jnp.float32,
    )
    back_message = jnp.take(back_summed, edge_target, axis=2) * inverse_avg
    weighted_back = back_message * weighted[None]
    back_harmonic = jnp.sum(weighted_back * spread, axis=1)
    component = weighted_back * harmonic[:, None, :]
    back_radial = jnp.stack(
        [jnp.sum(component[first:last], axis=0) for first, last in DEGREE_SLICES]
    )
    back_radial = back_radial.reshape(4 * channels, slot_count).astype(jnp.bfloat16)
    back_weighted = (
        jnp.sum(back_message * spread * harmonic[:, None, :], axis=0) * live_mask[None, :]
    )
    grad_out = outer_sum(act_three, back_radial)
    back_pre_three = (project_back(w_out, back_radial) * silu_slope(pre_three)).astype(jnp.bfloat16)
    grad_hidden_two = outer_sum(act_two, back_pre_three)
    back_pre_two = (project_back(w_hidden[1], back_pre_three) * silu_slope(pre_two)).astype(
        jnp.bfloat16
    )
    grad_hidden_one = outer_sum(act_one, back_pre_two)
    back_pre_one = (project_back(w_hidden[0], back_pre_two) * silu_slope(pre_one)).astype(
        jnp.bfloat16
    )
    grad_in = outer_sum(bessel_low, back_pre_one)
    back_bessel = project_back(w_in, back_pre_one)
    unused_value, geometry_back = jax.vjp(geometry, edge_vectors)
    (back_relative,) = geometry_back((back_bessel, back_harmonic))
    ext_width = extended.shape[1]
    feature_back = (
        jnp.zeros((channels, ext_width), jnp.float32).at[:, edge_source].add(back_weighted)
    )
    position_back = jnp.zeros((3, ext_width), jnp.float32).at[:, edge_source].add(back_relative)
    position_back = position_back.at[:, edge_target].add(-back_relative)
    stacked_back = jnp.concatenate([feature_back, position_back], axis=0)
    owned = stacked_back[:, :local_atoms].at[:channels].add(back_local)
    for axis_pos in range(3):
        for direction in (1, -1):
            face_row = 2 * axis_pos + (0 if direction == 1 else 1)
            first_col = local_atoms + face_row * halo_width
            returned = backward_face(
                stacked_back[:, first_col : first_col + halo_width], axis_pos, -direction
            )
            owned = owned.at[:, halo_index[face_row]].add(returned)
    feature_grad = owned[:channels]
    position_grad = owned[channels:]
    grads = (
        grad_in,
        jnp.stack([grad_hidden_one, grad_hidden_two]),
        grad_out,
        grad_degree,
        grad_species,
        grad_readout,
    )
    summed_grads = lax.psum(
        (grads[0], grads[1], grads[2], grads[3], grads[4], grads[5]), ("gx", "gy", "gz")
    )
    updated = [
        adamw_update(
            masters[member], moments[member], squares[member], summed_grads[member], RATES[member]
        )
        for member in range(6)
    ]
    new_weights = [entry[0] for entry in updated]
    new_moments = [entry[1] for entry in updated]
    new_squares = [entry[2] for entry in updated]
    return (
        site_energy,
        feature_grad,
        position_grad,
        new_weights[0],
        new_weights[1],
        new_weights[2],
        new_weights[3],
        new_weights[4],
        new_weights[5],
        new_moments[0],
        new_moments[1],
        new_moments[2],
        new_moments[3],
        new_moments[4],
        new_moments[5],
        new_squares[0],
        new_squares[1],
        new_squares[2],
        new_squares[3],
        new_squares[4],
        new_squares[5],
    )


def solution(mesh):
    in_specs = (
        P(None, ("gx", "gy", "gz")),
        P(None, ("gx", "gy", "gz")),
        P(("gx", "gy", "gz")),
        P(("gx", "gy", "gz")),
        P(("gx", "gy", "gz")),
        P(None, ("gx", "gy", "gz")),
        P(("gx", "gy", "gz")),
        P(("gx", "gy", "gz")),
        P(),
        P(),
        P(),
        P(),
        P(),
        P(),
        P(),
        P(),
        P(),
        P(),
        P(),
        P(),
        P(),
        P(),
        P(),
        P(),
        P(),
        P(),
    )
    out_specs = (
        P(("gx", "gy", "gz")),
        P(None, ("gx", "gy", "gz")),
        P(None, ("gx", "gy", "gz")),
        P(),
        P(),
        P(),
        P(),
        P(),
        P(),
        P(),
        P(),
        P(),
        P(),
        P(),
        P(),
        P(),
        P(),
        P(),
        P(),
        P(),
        P(),
    )
    return jax.shard_map(
        on_device, mesh=mesh, in_specs=in_specs, out_specs=out_specs, check_vma=False
    )
```

profile of v0, /device:TPU:0, one launch (start us, length us, event | category | flops | bytes accessed | tf_op | source)
XLA Modules:
  0.0 732.7 jit_solution(12279158902534513967)
XLA Ops:
  10.6 2.9 collective-permute-start
  17.8 1.7 collective-permute-start.3
  20.9 2.1 collective-permute-start.4
  33.7 2.0 multiply_convert_fusion.4
  46.3 2.4 copy.265
  50.0 1.9 copy.266
  51.9 1.6 copy.276
  53.5 2.3 collective-permute-start.5
  59.7 6.2 gather_fusion
  71.8 11.2 %fusion.4 = f32[2048,16,64]{2,1,0:T(8,128)} fusion(f32[7,64,2048]{1,0,2:T(8,128)S(1)} %broadcast_in_dim.50, f32[5,64,2048]{1,0,2:T(8,128)S(1)} %broadcast_in_dim.49, f32[3,64,2048]{1,0,2:T(4,128)S(1)} %broadcast_in_dim.48, f32[1,64,2048]{1,0,2:T(1,128)} %copy.266, f32[64,2048]{0,1:T(8,128)} %multiply_bitcast_fusion, f32[16,2048]{0,1:T(8,128)S(1)} %copy.267), kind=kLoop, calls=%fused_computation.23 | loop fusion | flops 10485760 | bytes 17432576 | tf_op jit(solution)/shard_map/mul | solution.py:199
  83.1 2.3 broadcast_in_dim.46
  85.4 247.8 %scatter_fusion = f32[16,64,512]{1,0,2:T(8,128)} fusion(f32[16,64,512]{1,0,2:T(8,128)} %broadcast_in_dim.46, s32[2048]{0:T(1024)S(1)} %copy-done.45, f32[2048,16,64]{2,1,0:T(8,128)} %fusion.4), kind=kCustom, calls=%fused_computation.8 | custom fusion | flops 2097152 | bytes 25174016 | tf_op jit(solution)/shard_map/scatter-add | solution.py:201
  333.2 3.8 copy.275
  337.0 1.9 multiply_convert_fusion
  348.6 4.9 copy.281
  353.5 21.1 %gather_fusion.1 = f32[2048,16,64]{2,1,0:T(8,128)} fusion(f32[16,64,512]{1,0,2:T(8,128)} %copy.281, s32[2048]{0:T(1024)S(1)} %copy-done.44), kind=kCustom, calls=%fused_computation.7 | custom fusion | bytes 16785408 | tf_op jit(solution)/shard_map/jit(_take)/gather | solution.py:283
  374.5 66.2 %fusion.6 = (f32[16,2048]{0,1:T(8,128)S(1)}, f32[64,2048]{0,1:T(8,128)}, f32[16,64,2048]{1,0,2:T(8,128)}) fusion(f32[7,64,2048]{1,0,2:T(8,128)} %copy-done.1, f32[5,64,2048]{1,0,2:T(8,128)} %copy-done, f32[3,64,2048]{1,0,2:T(4,128)} %copy-done.2, f32[1,64,2048]{1,0,2:T(1,128)} %copy.266, f32[2048,16,64]{2,1,0:T(8,128)} %gather_fusion.1, ...), kind=kLoop, calls=%fused_computation.25 | loop fusion | flops 25001984 | bytes 26478592 | tf_op jit(solution)/shard_map/reduce_sum | solution.py:285
  440.8 13.6 %slice_reduce_fusion.2 = bf16[64,2048]{0,1:T(8,128)(2,1)S(1)} fusion(f32[16,64,2048]{1,0,2:T(8,128)} %get-tuple-element.229), kind=kLoop, calls=%fused_computation.32 | loop fusion | flops 262144 | bytes 1835008 | tf_op jit(solution)/shard_map/reduce_sum | solution.py:288
  454.3 14.3 %slice_reduce_fusion.1 = bf16[64,2048]{0,1:T(8,128)(2,1)S(1)} fusion(f32[16,64,2048]{1,0,2:T(8,128)} %get-tuple-element.229), kind=kLoop, calls=%fused_computation.31 | loop fusion | flops 524288 | bytes 2883584 | tf_op jit(solution)/shard_map/reduce_sum | solution.py:288
  468.6 13.2 %slice_reduce_fusion = bf16[64,2048]{0,1:T(8,128)(2,1)S(1)} fusion(f32[16,64,2048]{1,0,2:T(8,128)} %get-tuple-element.229), kind=kLoop, calls=%fused_computation.30 | loop fusion | flops 786432 | bytes 3932160 | tf_op jit(solution)/shard_map/reduce_sum | solution.py:288
  481.9 4.6 slice.411
  486.6 2.0 copy.300
  488.8 2.0 copy.301
  491.0 2.0 copy.302
  493.0 7.5 %pad_maximum_fusion.2 = bf16[4,64,2048]{1,0,2:T(4,128)(2,1)S(1)} fusion(bf16[1,64,2048]{1,0,2:T(2,128)(2,1)} %copy.302, bf16[1,64,2048]{1,0,2:T(2,128)(2,1)} %copy.301, bf16[1,64,2048]{1,0,2:T(2,128)(2,1)} %copy.300, bf16[1,64,2048]{1,0,2:T(2,128)(2,1)} %slice.411), kind=kLoop, calls=%fused_computation.48 | loop fusion | flops 4194304 | bytes 2097152 | tf_op jit(solution)/shard_map/stack | solution.py:287
  500.5 2.5 copy.303
  503.1 2.5 fusion.120
  505.7 1.8 fusion.12
  512.6 8.9 %fusion.127 = (f32[1,2048]{0,1:T(8,128)}, f32[1,2048]{0,1:T(8,128)}, f32[1,2048]{0,1:T(8,128)}, f32[1,2048]{0,1:T(8,128)}, f32[1,2048]{0,1:T(8,128)S(1)}, /*inde...) fusion(f32[16,2048]{0,1:T(8,128)S(1)} %get-tuple-element.181), kind=kLoop, calls=%fused_computation.341 | loop fusion | bytes 245760 | tf_op jit(solution)/shard_map/transpose(jvp())/unstack | solution.py:38
  521.5 1.6 copy.317
  523.1 1.6 copy.318
  524.7 1.6 copy.319
  526.3 1.6 copy.320
  528.2 2.3 copy.322
  532.0 1.6 copy.324
  533.6 2.2 copy.325
  535.7 2.1 copy.326
  538.8 1.6 copy.328
  548.4 12.0 %scatter_custom_fusion.2 = f32[3,1280]{0,1:T(8,128)S(1)} fusion(s32[2048]{0:T(1024)} %get-tuple-element.279, f32[2048,3]{1,0:T(8,128)} %copy.304, f32[]{:T(128)} %constant.63.clone.1), kind=kCustom, calls=%fused_computation.101 | custom fusion | flops 6144 | bytes 15872 | tf_op jit(solution)/shard_map/scatter-add | solution.py:312
  560.4 13.0 %scatter_custom_fusion.1 = f32[64,1280]{0,1:T(8,128)S(1)} fusion(s32[2048]{0:T(1024)} %get-tuple-element.279, f32[64,2048]{0,1:T(8,128)S(1)} %copy-done.3, f32[2048]{0:T(1024)S(1)} %get-tuple-element.305, f32[]{:T(128)} %constant.63.clone.1), kind=kCustom, calls=%fused_computation.72 | custom fusion | flops 262144 | bytes 860672 | tf_op jit(solution)/shard_map/scatter-add | solution.py:310
  573.5 12.0 %scatter_fusion.1 = f32[3,1280]{0,1:T(8,128)S(1)} fusion(f32[3,1280]{0,1:T(8,128)S(1)} %scatter_custom_fusion.2, s32[2048]{0:T(1024)} %get-tuple-element.273, f32[2048,3]{1,0:T(8,128)S(1)} %copy.305), kind=kCustom, calls=%fused_computation.11 | custom fusion | flops 6144 | bytes 81920 | tf_op jit(solution)/shard_map/scatter-add | solution.py:313
  586.4 1.7 collective-permute-start.6
  590.2 2.0 collective-permute-start.10
  595.2 39.8 %all-reduce.3 = (f32[8,64]{1,0:T(8,128)S(1)}, f32[2,64,64]{2,1,0:T(8,128)S(1)}, f32[2,64]{1,0:T(2,128)S(1)}) all-reduce(f32[8,64]{1,0:T(8,128)S(1)} %copy-done.62, f32[2,64,64]{2,1,0:T(8,128)S(1)} %pad_maximum_fusion.6, f32[2,64]{1,0:T(2,128)S(1)} %pad_maximum_fusion.7), channel_id=1, replica_groups=mesh['gx'=2,'gy'=4,'gz'=4] {'gx','gy','gz'}, use_global_device_ids=true, to_apply=%region_24.26 | all-reduce | flops 8832 | bytes 70656 | tf_op jit(solution)/shard_map/psum | solution.py:334
  638.5 2.0 collective-permute-start.11
  652.6 68.0 %all-reduce.7.cloned.1.call-done = (f32[64,256]{1,0:T(8,128)}, f32[4,64,64]{2,1,0:T(8,128)}, f32[4,64,64]{2,1,0:T(8,128)}) async-done(((f32[64,256]{1,0:T(8,128)}, f32[4,64,64]{2,1,0:T(8,128)}, f32[4,64,64]{2,1,0:T(8,128)}), (f32[64,256]{1,0:T(8,128)}, f32[4,64,64]{2,1,0:T(8,128)}, f32[4,64,64]{2,1,0:T(8,128)})) %all-reduce.7.cloned.1.call-update) | async-done | bytes 196624 | tf_op jit(solution)/shard_map/psum | solution.py:334
  720.6 1.7 multiply_subtract_fusion
  722.3 1.7 multiply_subtract_fusion.1
  (281 shorter events, 89.4 us)
Async XLA Ops:
  7.2 32.0 %copy-start.30 = (f32[64,256]{1,0:T(8,128)S(1)}, f32[64,256]{1,0:T(8,128)}, u32[]{:S(2)}) copy-start(f32[64,256]{1,0:T(8,128)} %param.40) | copy-start | bytes 196612
  7.2 713.4 %all-reduce.7.cloned.1.call-start = ((), (), s32[]{:S(2)}) async-start(), calls=%async_computation | async-start | bytes 655360 | tf_op jit(solution)/shard_map/psum | solution.py:334
  10.6 42.9 %collective-permute-start = (bf16[64,128]{0,1:T(8,128)(2,1)}, bf16[64,128]{0,1:T(8,128)(2,1)}, u32[]{:S(2)}, u32[]{:S(2)}) collective-permute-start(bf16[64,128]{0,1:T(8,128)(2,1)} %select_bitcast_fusion.5), channel_id=1, source_target_pairs={{0,16},{16,0},{1,17},{17,1},{2,18},{18,2},{3,19},{19,3},{4,20},{20... | collective-permute-start | bytes 49160 | tf_op jit(solution)/shard_map/ppermute | solution.py:32
  14.9 41.7 %collective-permute-start.1 = (bf16[64,128]{0,1:T(8,128)(2,1)}, bf16[64,128]{0,1:T(8,128)(2,1)}, u32[]{:S(2)}, u32[]{:S(2)}) collective-permute-start(bf16[64,128]{0,1:T(8,128)(2,1)} %select_bitcast_fusion.4), channel_id=1, source_target_pairs={{0,16},{16,0},{1,17},{17,1},{2,18},{18,2},{3,19},{19,3},{4,20},{20... | collective-permute-start | bytes 49160 | tf_op jit(solution)/shard_map/ppermute | solution.py:32
  16.3 41.0 %collective-permute-start.2 = (bf16[64,128]{0,1:T(8,128)(2,1)}, bf16[64,128]{0,1:T(8,128)(2,1)}, u32[]{:S(2)}, u32[]{:S(2)}) collective-permute-start(bf16[64,128]{0,1:T(8,128)(2,1)} %select_bitcast_fusion.3), channel_id=1, source_target_pairs={{0,4},{4,8},{8,12},{12,0},{1,5},{5,9},{9,13},{13,1},{2,6},{6,10},{... | collective-permute-start | bytes 49160 | tf_op jit(solution)/shard_map/ppermute | solution.py:32
  17.8 40.3 %collective-permute-start.3 = (bf16[64,128]{0,1:T(8,128)(2,1)}, bf16[64,128]{0,1:T(8,128)(2,1)}, u32[]{:S(2)}, u32[]{:S(2)}) collective-permute-start(bf16[64,128]{0,1:T(8,128)(2,1)} %select_bitcast_fusion.2), channel_id=1, source_target_pairs={{0,12},{4,0},{8,4},{12,8},{1,13},{5,1},{9,5},{13,9},{2,14},{6,2},{... | collective-permute-start | bytes 49160 | tf_op jit(solution)/shard_map/ppermute | solution.py:32
  20.9 38.0 %collective-permute-start.4 = (bf16[64,128]{0,1:T(8,128)(2,1)}, bf16[64,128]{0,1:T(8,128)(2,1)}, u32[]{:S(2)}, u32[]{:S(2)}) collective-permute-start(bf16[64,128]{0,1:T(8,128)(2,1)} %select_bitcast_fusion.1), channel_id=1, source_target_pairs={{0,1},{1,2},{2,3},{3,0},{4,5},{5,6},{6,7},{7,4},{8,9},{9,10},{10,1... | collective-permute-start | bytes 49160 | tf_op jit(solution)/shard_map/ppermute | solution.py:32
  23.8 8.3 %copy-start.38 = (f32[2048]{0:T(1024)}, f32[2048]{0:T(1024)S(1)}, u32[]{:S(2)}) copy-start(f32[2048]{0:T(1024)S(1)} %multiply_reduce_fusion.6) | copy-start | bytes 24580
  24.4 15.2 %copy-start.52 = (f32[2048]{0:T(1024)}, f32[2048]{0:T(1024)S(1)}, u32[]{:S(2)}) copy-start(f32[2048]{0:T(1024)S(1)} %get-tuple-element.277) | copy-start | bytes 24580
  25.4 14.3 %copy-start.65 = (f32[8]{0:T(128)}, f32[8]{0:T(128)S(1)}, u32[]{:S(2)}) copy-start(f32[8]{0:T(128)S(1)} %convert_multiply_fusion) | copy-start | bytes 100
  32.9 33.0 %copy-start.48 = (pred[2048]{0:T(1024)(128)(4,1)}, pred[2048]{0:T(1024)(128)(4,1)S(1)}, u32[]{:S(2)}) copy-start(pred[2048]{0:T(1024)(128)(4,1)S(1)} %get-tuple-element.306) | copy-start | bytes 6148
  53.5 6.2 collective-permute-start.5
  70.6 12.5 %copy-start.1 = (f32[7,64,2048]{1,0,2:T(8,128)}, f32[7,64,2048]{1,0,2:T(8,128)S(1)}, u32[]{:S(2)}) copy-start(f32[7,64,2048]{1,0,2:T(8,128)S(1)} %broadcast_in_dim.50) | copy-start | bytes 11010052
  71.8 11.2 %copy-start.2 = (f32[3,64,2048]{1,0,2:T(4,128)}, f32[3,64,2048]{1,0,2:T(4,128)S(1)}, u32[]{:S(2)}) copy-start(f32[3,64,2048]{1,0,2:T(4,128)S(1)} %broadcast_in_dim.48) | copy-start | bytes 4718596
  353.5 21.1 %copy-start.51 = (pred[2048]{0:T(1024)(128)(4,1)S(1)}, pred[2048]{0:T(1024)(128)(4,1)}, u32[]{:S(2)}) copy-start(pred[2048]{0:T(1024)(128)(4,1)} %compare_and_fusion) | copy-start | bytes 6148
  500.5 7.0 copy-start.9
  500.5 7.0 copy-start.11
  500.5 7.0 copy-start.29
  500.5 7.0 copy-start.50
  500.5 7.0 copy-start.57
  503.1 6.2 copy-start.37
  521.5 6.3 copy-start.7
  528.2 13.9 %copy-start.6 = (f32[1,2048]{0,1:T(8,128)S(1)}, f32[1,2048]{0,1:T(8,128)}, u32[]{:S(2)}) copy-start(f32[1,2048]{0,1:T(8,128)} %get-tuple-element.242) | copy-start | bytes 24580
  532.0 10.8 %copy-start.58 = (f32[8,64]{1,0:T(8,128)S(1)}, f32[8,64]{1,0:T(8,128)}, u32[]{:S(2)}) copy-start(f32[8,64]{1,0:T(8,128)} %param.38) | copy-start | bytes 6148
  532.0 10.8 %copy-start.67 = (f32[8]{0:T(128)S(1)}, f32[8]{0:T(128)}, u32[]{:S(2)}) copy-start(f32[8]{0:T(128)} %copy-done.65) | copy-start | bytes 100
  533.6 11.6 %copy-start.20 = (f32[3,2048]{1,0:T(4,128)S(1)}, f32[3,2048]{1,0:T(4,128)}, u32[]{:S(2)}) copy-start(f32[3,2048]{1,0:T(4,128)} %param.31) | copy-start | bytes 73732
  538.8 21.6 %copy-start.3 = (f32[64,2048]{0,1:T(8,128)S(1)}, f32[64,2048]{0,1:T(8,128)}, u32[]{:S(2)}) copy-start(f32[64,2048]{0,1:T(8,128)} %get-tuple-element.182) | copy-start | bytes 1572868
  544.1 44.1 %copy-start.14 = (f32[4,64,64]{2,1,0:T(8,128)S(1)}, f32[4,64,64]{2,1,0:T(8,128)}, u32[]{:S(2)}) copy-start(f32[4,64,64]{2,1,0:T(8,128)} %param.42) | copy-start | bytes 196612
  548.1 88.5 %copy-start.59 = (f32[8,64]{1,0:T(8,128)S(1)}, f32[8,64]{1,0:T(8,128)}, u32[]{:S(2)}) copy-start(f32[8,64]{1,0:T(8,128)} %param.38) | copy-start | bytes 6148
  548.1 88.5 %copy-start.60 = (f32[8,64]{1,0:T(8,128)S(1)}, f32[8,64]{1,0:T(8,128)}, u32[]{:S(2)}) copy-start(f32[8,64]{1,0:T(8,128)} %param.44) | copy-start | bytes 6148
  573.5 21.7 %copy-start.62 = (f32[8,64]{1,0:T(8,128)S(1)}, f32[8,64]{1,0:T(8,128)}, u32[]{:S(2)}) copy-start(f32[8,64]{1,0:T(8,128)} %fusion.77) | copy-start | bytes 6148
  573.5 61.6 %copy-start.25 = (f32[2,64,64]{2,1,0:T(8,128)S(1)}, f32[2,64,64]{2,1,0:T(8,128)}, u32[]{:S(2)}) copy-start(f32[2,64,64]{2,1,0:T(8,128)} %param.39) | copy-start | bytes 98308
  573.5 61.6 %copy-start.39 = (f32[2,64,64]{2,1,0:T(8,128)S(1)}, f32[2,64,64]{2,1,0:T(8,128)}, u32[]{:S(2)}) copy-start(f32[2,64,64]{2,1,0:T(8,128)} %param.45) | copy-start | bytes 98308
  573.5 63.1 %copy-start.61 = (f32[8,64]{1,0:T(8,128)S(1)}, f32[8,64]{1,0:T(8,128)}, u32[]{:S(2)}) copy-start(f32[8,64]{1,0:T(8,128)} %param.50) | copy-start | bytes 6148
  586.4 134.2 %copy-start.32 = (f32[4,64,64]{2,1,0:T(8,128)S(1)}, f32[4,64,64]{2,1,0:T(8,128)}, u32[]{:S(2)}) copy-start(f32[4,64,64]{2,1,0:T(8,128)} %param.48) | copy-start | bytes 196612
  586.4 134.2 %copy-start.33 = (f32[4,64,64]{2,1,0:T(8,128)S(1)}, f32[4,64,64]{2,1,0:T(8,128)}, u32[]{:S(2)}) copy-start(f32[4,64,64]{2,1,0:T(8,128)} %param.54) | copy-start | bytes 196612
  586.4 52.2 %collective-permute-start.6 = (f32[67,128]{0,1:T(8,128)}, f32[67,128]{0,1:T(8,128)S(1)}, u32[]{:S(2)}, u32[]{:S(2)}) collective-permute-start(f32[67,128]{0,1:T(8,128)} %get-tuple-element.236), channel_id=1, source_target_pairs={{0,16},{16,0},{1,17},{17,1},{2,18},{18,2},{3,19},{19,3},{4,20},{20... | collective-permute-start | bytes 102920 | tf_op jit(solution)/shard_map/ppermute | solution.py:32
  588.2 134.1 %copy-start.19 = (f32[4,64,64]{2,1,0:T(8,128)S(1)}, f32[4,64,64]{2,1,0:T(8,128)}, u32[]{:S(2)}) copy-start(f32[4,64,64]{2,1,0:T(8,128)} %param.41) | copy-start | bytes 196612
  588.2 134.1 %copy-start.34 = (f32[4,64,64]{2,1,0:T(8,128)S(1)}, f32[4,64,64]{2,1,0:T(8,128)}, u32[]{:S(2)}) copy-start(f32[4,64,64]{2,1,0:T(8,128)} %param.47) | copy-start | bytes 196612
  588.2 134.1 %copy-start.35 = (f32[4,64,64]{2,1,0:T(8,128)S(1)}, f32[4,64,64]{2,1,0:T(8,128)}, u32[]{:S(2)}) copy-start(f32[4,64,64]{2,1,0:T(8,128)} %param.53) | copy-start | bytes 196612
  589.3 54.1 %collective-permute-start.7 = (f32[67,128]{0,1:T(8,128)}, f32[67,128]{0,1:T(8,128)S(1)}, u32[]{:S(2)}, u32[]{:S(2)}) collective-permute-start(f32[67,128]{0,1:T(8,128)} %get-tuple-element.237), channel_id=1, source_target_pairs={{0,16},{16,0},{1,17},{17,1},{2,18},{18,2},{3,19},{19,3},{4,20},{20... | collective-permute-start | bytes 102920 | tf_op jit(solution)/shard_map/ppermute | solution.py:32
  589.7 55.2 %collective-permute-start.8 = (f32[67,128]{0,1:T(8,128)}, f32[67,128]{0,1:T(8,128)S(1)}, u32[]{:S(2)}, u32[]{:S(2)}) collective-permute-start(f32[67,128]{0,1:T(8,128)} %get-tuple-element.238), channel_id=1, source_target_pairs={{0,12},{4,0},{8,4},{12,8},{1,13},{5,1},{9,5},{13,9},{2,14},{6,2},{... | collective-permute-start | bytes 102920 | tf_op jit(solution)/shard_map/ppermute | solution.py:32
  589.7 56.7 %collective-permute-start.9 = (f32[67,128]{0,1:T(8,128)S(1)}, f32[67,128]{0,1:T(8,128)S(1)}, u32[]{:S(2)}, u32[]{:S(2)}) collective-permute-start(f32[67,128]{0,1:T(8,128)S(1)} %get-tuple-element.239), channel_id=1, source_target_pairs={{0,4},{4,8},{8,12},{12,0},{1,5},{5,9},{9,13},{13,1},{2,6},{6,10},{... | collective-permute-start | bytes 102920 | tf_op jit(solution)/shard_map/ppermute | solution.py:32
  590.2 57.7 %collective-permute-start.10 = (f32[67,128]{0,1:T(8,128)S(1)}, f32[67,128]{0,1:T(8,128)S(1)}, u32[]{:S(2)}, u32[]{:S(2)}) collective-permute-start(f32[67,128]{0,1:T(8,128)S(1)} %get-tuple-element.240), channel_id=1, source_target_pairs={{0,3},{1,0},{2,1},{3,2},{4,7},{5,4},{6,5},{7,6},{8,11},{9,8},{10,9... | collective-permute-start | bytes 102920 | tf_op jit(solution)/shard_map/ppermute | solution.py:32
  595.2 128.9 %copy-start.31 = (f32[64,256]{1,0:T(8,128)S(1)}, f32[64,256]{1,0:T(8,128)}, u32[]{:S(2)}) copy-start(f32[64,256]{1,0:T(8,128)} %param.40) | copy-start | bytes 196612
  595.2 128.9 %copy-start.40 = (f32[64,256]{1,0:T(8,128)S(1)}, f32[64,256]{1,0:T(8,128)}, u32[]{:S(2)}) copy-start(f32[64,256]{1,0:T(8,128)} %param.46) | copy-start | bytes 196612
  595.2 128.9 %copy-start.41 = (f32[64,256]{1,0:T(8,128)S(1)}, f32[64,256]{1,0:T(8,128)}, u32[]{:S(2)}) copy-start(f32[64,256]{1,0:T(8,128)} %param.52) | copy-start | bytes 196612
  638.5 10.9 %collective-permute-start.11 = (f32[67,128]{0,1:T(8,128)S(1)}, f32[67,128]{0,1:T(8,128)S(1)}, u32[]{:S(2)}, u32[]{:S(2)}) collective-permute-start(f32[67,128]{0,1:T(8,128)S(1)} %get-tuple-element.235), channel_id=1, source_target_pairs={{0,1},{1,2},{2,3},{3,0},{4,5},{5,6},{6,7},{7,4},{8,9},{9,10},{10,1... | collective-permute-start | bytes 102920 | tf_op jit(solution)/shard_map/ppermute | solution.py:32
  (36 other events, 143.3 us)
Sparse Core Ops, SparseCore 0:
  595.3 125.2 all-reduce.6
where the time goes:
time: 742 us; the launch traced here: 733 us
  other arithmetic  459 us (62%)
  local copies, waits for them, and re-layouts  113 us (15%)
  waiting for transfers between devices  68 us (9%)
  blocking collectives  39.8 us (5%)
  matrix products  20.8 us (3%)
  between operations  16 us (2%)
  starting transfers between devices  15.8 us (2%)
    scatter-add x1, other arithmetic, on_device(): jnp.zeros((16, channels, local_atoms), jnp.float32).at[:, :, edge_target]  248 us
    psum x1, waiting for transfers between devices, on_device(): lax.psum((grads[0], grads[1], grads[2], grads[3], grads[4], grads[5]), ('...  68 us
    reduce_sum x1, other arithmetic, on_device(): back_harmonic = jnp.sum(weighted_back * spread, axis=1)  66.2 us
    reduce_sum x3, other arithmetic, on_device(): jnp.sum(component[first:last], axis=0)  41.1 us
    psum x1, blocking collectives, on_device(): lax.psum((grads[0], grads[1], grads[2], grads[3], grads[4], grads[5]), ('...  39.8 us
    unnamed x168, local copies, waits for them, and re-layouts  34.2 us
    gather x1, local copies, waits for them, and re-layouts, on_device(): back_message = jnp.take(back_summed, edge_target, axis=2) * inverse_avg  21.1 us
    ppermute x12, starting transfers between devices, shifted(): return lax.ppermute(value, axis, pairs)  15.7 us
  transfers between devices with their start and end apart: 13, of which 1 were waited for; matrix products, arithmetic and copies ran while one was open for 8% of the time, Pallas kernels for 0%

commit v1 on v0

v1 whole, which is shorter than its diff:
```python
import math

import jax
import jax.numpy as jnp
from jax import lax
from jax.experimental import pallas as pl
from jax.experimental.pallas import tpu as pltpu
from jax.sharding import PartitionSpec as P

NBASIS = 8
STEP = 10
CUTOFF = 5.0
BESSEL_NORM = math.sqrt(2.0 / 5.0)
SQRT3 = math.sqrt(3.0)
SQRT5 = math.sqrt(5.0)
SQRT7 = math.sqrt(7.0)
SQRT15 = math.sqrt(15.0)
CUBIC_A = math.sqrt(35.0 / 8.0)
CUBIC_B = math.sqrt(105.0)
CUBIC_C = math.sqrt(21.0 / 8.0)
BETA_ONE = 0.9
BETA_TWO = 0.999
EPSILON = 1e-08
DECAY = 0.01
RATES = (2.0, 0.2, 0.125, 0.125, 0.125, 0.125)
DEGREE_SLICES = ((0, 1), (1, 4), (4, 9), (9, 16))
DEGREE_OF = tuple(d for d, (a, b) in enumerate(DEGREE_SLICES) for _ in range(a, b))
AXES = ("gx", "gy", "gz")
F32 = jnp.float32
BF16 = jnp.bfloat16
LANES = 128
TILE = 256
BACK_ROWS = 80
PACK_ROWS = 456
VMEM_LIMIT = 50 * 1024 * 1024


def dot_nn(left, right):
    return lax.dot_general(left, right, (((1,), (0,)), ((), ())), preferred_element_type=F32)


def dot_nt(left, right):
    return lax.dot_general(left, right, (((1,), (1,)), ((), ())), preferred_element_type=F32)


def dot_tn(left, right):
    return lax.dot_general(left, right, (((0,), (0,)), ((), ())), preferred_element_type=F32)


def halves(values):
    high = values.astype(BF16)
    return high, (values - high.astype(F32)).astype(BF16)


def one_hot(row, count, base=0):
    place = lax.broadcasted_iota(jnp.int32, (count, row.shape[1]), 0) + base
    return jnp.where(place == row, 1.0, 0.0).astype(BF16)


def index_row(rows, first, width):
    start = first // LANES
    return jnp.concatenate(
        [rows[start + n : start + n + 1, :] for n in range(width // LANES)], axis=1
    )


def live_sources(source_ref, count_ref):
    rows = source_ref[...]
    slot = lax.broadcasted_iota(jnp.int32, rows.shape, 0) * LANES + lax.broadcasted_iota(
        jnp.int32, rows.shape, 1
    )
    return jnp.where(slot < count_ref[0], rows, -1)


def column_of(row):
    size = row.shape[1]
    eye = lax.broadcasted_iota(jnp.int32, (size, size), 0) == lax.broadcasted_iota(
        jnp.int32, (size, size), 1
    )
    return jnp.sum(jnp.where(eye, row, 0.0), axis=1, keepdims=True)


def row_of(column):
    size = column.shape[0]
    eye = lax.broadcasted_iota(jnp.int32, (size, size), 0) == lax.broadcasted_iota(
        jnp.int32, (size, size), 1
    )
    return jnp.sum(jnp.where(eye, column, 0.0), axis=0, keepdims=True)


def pick_faces_kernel(feats_ref, halo_ref, *face_refs):
    channels, atoms = feats_ref.shape
    feats = feats_ref[...]
    halo = halo_ref[...]
    face = 0
    for ref in face_refs:
        for part in range(ref.shape[0] // channels):
            picked = dot_nn(feats, one_hot(halo[face : face + 1, :], atoms))
            ref[part * channels : (part + 1) * channels, :] = picked.astype(BF16)
            face += 1


def radial_kernel(
    count_ref,
    feats_ref,
    vectors_ref,
    source_ref,
    species_ref,
    w_in_ref,
    w_hidden_ref,
    w_out_ref,
    w_species_ref,
    own_ref,
    harm_ref,
    geo_ref,
    slope_b_ref,
    bessel_ref,
    act_ref,
    slope_ref,
    radial_ref,
    self_ref,
):
    channels, atoms = feats_ref.shape
    slots = vectors_ref.shape[1]
    vectors = vectors_ref[...]
    vx, vy, vz = vectors[0:1, :], vectors[1:2, :], vectors[2:3, :]
    dist = jnp.sqrt(vx * vx + vy * vy + vz * vz)
    inverse = 1.0 / dist
    x, y, z = vx / dist, vy / dist, vz / dist
    scaled = dist / CUTOFF
    square = scaled * scaled
    five = square * square * scaled
    six = square * square * square
    envelope = 1.0 - 28.0 * six + 48.0 * six * scaled - 21.0 * six * scaled * scaled
    slope_env = (-168.0 * five + 336.0 * six - 168.0 * six * scaled) / CUTOFF
    freq = (lax.broadcasted_iota(jnp.int32, (NBASIS, 1), 0) + 1).astype(F32) * (math.pi / CUTOFF)
    angle = freq * dist
    sine, cosine = jnp.sin(angle), jnp.cos(angle)
    bessel = BESSEL_NORM * sine / dist * envelope
    slope_b_ref[...] = (
        BESSEL_NORM
        * inverse
        * ((freq * cosine - sine * inverse) * envelope + sine * slope_env)
    )
    zz = z * z
    harm_ref[...] = jnp.concatenate(
        [
            jnp.ones_like(x),
            SQRT3 * x,
            SQRT3 * y,
            SQRT3 * z,
            SQRT15 * x * y,
            SQRT15 * y * z,
            0.5 * SQRT5 * (3.0 * zz - 1.0),
            SQRT15 * x * z,
            0.5 * SQRT15 * (x * x - y * y),
            CUBIC_A * y * (3.0 * x * x - y * y),
            CUBIC_B * x * y * z,
            CUBIC_C * y * (5.0 * zz - 1.0),
            0.5 * SQRT7 * z * (5.0 * zz - 3.0),
            CUBIC_C * x * (5.0 * zz - 1.0),
            0.5 * CUBIC_B * z * (x * x - y * y),
            CUBIC_A * x * (x * x - 3.0 * y * y),
        ],
        axis=0,
    )
    geo_ref[0:3, :] = jnp.concatenate([x, y, z], axis=0)
    geo_ref[3:4, :] = inverse
    w_in = w_in_ref[...].astype(BF16)
    low = bessel.astype(BF16)
    bessel_ref[...] = low
    weights = [w_in, w_hidden_ref[0].astype(BF16), w_hidden_ref[1].astype(BF16)]
    for layer, weight in enumerate(weights):
        pre = dot_tn(weight, low)
        logistic = jax.nn.sigmoid(pre)
        low = (pre * logistic).astype(BF16)
        act_ref[layer] = low
        slope_ref[layer] = logistic * (1.0 + pre * (1.0 - logistic))
    radial_ref[...] = dot_tn(w_out_ref[...].astype(BF16), low)

    feats = feats_ref[...]
    kinds = w_species_ref.shape[0]
    species = species_ref[...]
    species_row = jnp.concatenate(
        [species[n : n + 1, :] for n in range(species.shape[0])], axis=1
    )
    total = jnp.zeros((channels, atoms), F32)
    for kind in range(kinds):
        masked = jnp.where(species_row == kind, feats.astype(F32), 0.0).astype(BF16)
        total += dot_tn(w_species_ref[kind].astype(BF16), masked)
    self_ref[...] = total

    sources = live_sources(source_ref, count_ref)
    for first in range(0, slots, TILE):
        hot = one_hot(index_row(sources, first, TILE), atoms)
        own_ref[:, first : first + TILE] = dot_nn(feats, hot).astype(BF16)


def layer_kernel(
    scale,
    face_count,
    count_ref,
    *refs,
):
    face_in = refs[:face_count]
    (
        own_ref,
        harm_ref,
        geo_ref,
        slope_b_ref,
        bessel_ref,
        act_ref,
        slope_ref,
        radial_ref,
        self_ref,
        feats_ref,
        source_ref,
        target_ref,
        species_ref,
        cotangent_ref,
        w_in_ref,
        w_hidden_ref,
        w_out_ref,
        w_degree_ref,
        w_species_ref,
        readout_ref,
    ) = refs[face_count : face_count + 20]
    energy_ref, owned_ref, pack_ref = refs[face_count + 20 : face_count + 23]
    face_out = refs[face_count + 23 : 2 * face_count + 23]
    (
        weighted_ref,
        message_ref,
        summed_ref,
        low_ref,
        mixed_back_ref,
        mixed_radial_ref,
        part_ref,
        harm_back_ref,
        radial_back_ref,
        stack_ref,
        target_hot_ref,
        source_hot_ref,
    ) = refs[2 * face_count + 23 :]
    channels, atoms = feats_ref.shape
    slots = harm_ref.shape[1]
    kinds = w_species_ref.shape[0]
    extended = source_hot_ref.shape[0]
    harm_count = harm_ref.shape[0]
    w_degree = [w_degree_ref[d].astype(BF16) for d in range(4)]

    sources = live_sources(source_ref, count_ref)
    targets = target_ref[...]
    pieces = []
    for ref in face_in:
        for part in range(ref.shape[0] // channels):
            pieces.append(ref[part * channels : (part + 1) * channels, :])
    borrowed = jnp.concatenate(pieces, axis=1)
    for first in range(0, slots, TILE):
        cols = slice(first, first + TILE)
        hot = one_hot(index_row(sources, first, TILE), extended)
        source_hot_ref[:, cols] = hot
        target_hot_ref[:, cols] = one_hot(index_row(targets, first, TILE), atoms)
        weighted_ref[:, cols] = (
            own_ref[:, cols].astype(F32) + dot_nn(borrowed, hot[atoms:, :])
        ) * scale

    for first in range(0, slots, TILE):
        cols = slice(first, first + TILE)
        weighted = weighted_ref[:, cols]
        scaled = [radial_ref[d * channels : (d + 1) * channels, cols] * weighted for d in range(4)]
        for k in range(harm_count):
            high, rest = halves(scaled[DEGREE_OF[k]] * harm_ref[k : k + 1, cols])
            message_ref[k * channels : (k + 1) * channels, :TILE] = high
            message_ref[k * channels : (k + 1) * channels, TILE:] = rest
        hot = target_hot_ref[:, cols]
        added = dot_nt(message_ref[...], jnp.concatenate([hot, hot], axis=1))
        if first == 0:
            summed_ref[...] = added
        else:
            summed_ref[...] += added

    total_square = jnp.zeros((channels, atoms), F32)
    scalars = self_ref[...]
    for k in range(harm_count):
        rows = slice(k * channels, (k + 1) * channels)
        low = summed_ref[rows, :].astype(BF16)
        low_ref[rows, :] = low
        mixed = dot_tn(w_degree[DEGREE_OF[k]], low)
        if k == 0:
            scalars = scalars + mixed
        else:
            summed_ref[rows, :] = mixed
            total_square += mixed * mixed
    cotangent = cotangent_ref[...]
    cotangent = jnp.concatenate(
        [cotangent[n : n + 1, :] for n in range(cotangent.shape[0])], axis=1
    )
    readout_scalar = column_of(readout_ref[0:1, :])
    readout_square = column_of(readout_ref[1:2, :])
    gate = jax.nn.sigmoid(scalars)
    scalar_out = scalars * gate
    quadratic = total_square * (gate * gate)
    energy_ref[...] = jnp.sum(
        readout_scalar * scalar_out + readout_square * quadratic, axis=0, keepdims=True
    )
    grad_readout = jnp.concatenate(
        [
            row_of(jnp.sum(scalar_out * cotangent, axis=1, keepdims=True)),
            row_of(jnp.sum(quadratic * cotangent, axis=1, keepdims=True)),
            jnp.zeros((6, channels), F32),
        ],
        axis=0,
    )
    back_quad = 2.0 * (readout_square * cotangent) * gate
    back_scalars = (readout_scalar * cotangent) * (
        gate * (1.0 + scalars * (1.0 - gate))
    ) + back_quad * total_square * (gate * (1.0 - gate))
    back_self = back_scalars.astype(BF16)
    mixed_back_ref[0:channels, :] = back_self
    factor = back_quad * gate
    for k in range(1, harm_count):
        rows = slice(k * channels, (k + 1) * channels)
        mixed_back_ref[rows, :] = (summed_ref[rows, :] * factor).astype(BF16)
    grad_degree = []
    for first, last in DEGREE_SLICES:
        total = jnp.zeros((channels, channels), F32)
        for k in range(first, last):
            rows = slice(k * channels, (k + 1) * channels)
            total += dot_nt(low_ref[rows, :], mixed_back_ref[rows, :])
        grad_degree.append(total)
    species = species_ref[...]
    species_row = jnp.concatenate(
        [species[n : n + 1, :] for n in range(species.shape[0])], axis=1
    )
    feats = feats_ref[...].astype(F32)
    back_local = jnp.zeros((channels, atoms), F32)
    grad_species = []
    for kind in range(kinds):
        mask = species_row == kind
        grad_species.append(dot_nt(jnp.where(mask, feats, 0.0).astype(BF16), back_self))
        back_local += dot_nn(
            w_species_ref[kind].astype(BF16), jnp.where(mask, back_scalars, 0.0).astype(BF16)
        )

    for d in range(4):
        rows = slice(d * channels, (d + 1) * channels)
        high, rest = halves(radial_ref[rows, :] * weighted_ref[...])
        mixed_radial_ref[rows, :] = dot_tn(w_degree[d], high) + dot_tn(w_degree[d], rest)
    for first in range(0, slots, TILE):
        cols = slice(first, first + TILE)
        gathered = dot_nn(mixed_back_ref[...], target_hot_ref[:, cols])
        for d, (begin, end) in enumerate(DEGREE_SLICES):
            part = jnp.zeros((channels, TILE), F32)
            mixed_radial = mixed_radial_ref[d * channels : (d + 1) * channels, cols]
            for k in range(begin, end):
                piece = gathered[k * channels : (k + 1) * channels, :]
                part += piece * harm_ref[k : k + 1, cols]
                harm_back_ref[k : k + 1, cols] = jnp.sum(
                    piece * mixed_radial, axis=0, keepdims=True
                )
            part_ref[d * channels : (d + 1) * channels, cols] = part
    back_weighted = jnp.zeros((channels, slots), F32)
    for d in range(4):
        rows = slice(d * channels, (d + 1) * channels)
        high, rest = halves(part_ref[rows, :])
        mixed_part = dot_nn(w_degree[d], high) + dot_nn(w_degree[d], rest)
        radial_back_ref[rows, :] = (mixed_part * weighted_ref[...]).astype(BF16)
        back_weighted += mixed_part * radial_ref[rows, :]
    back_weighted = back_weighted * scale
    high, rest = halves(back_weighted)
    stack_ref[0:channels, :] = high
    stack_ref[BACK_ROWS : BACK_ROWS + channels, :] = rest

    radial_back = radial_back_ref[...]
    grad_out = dot_nt(act_ref[2], radial_back)
    back_pre = (dot_nn(w_out_ref[...].astype(BF16), radial_back) * slope_ref[2]).astype(BF16)
    grad_hidden_two = dot_nt(act_ref[1], back_pre)
    back_pre = (dot_nn(w_hidden_ref[1].astype(BF16), back_pre) * slope_ref[1]).astype(BF16)
    grad_hidden_one = dot_nt(act_ref[0], back_pre)
    back_pre = (dot_nn(w_hidden_ref[0].astype(BF16), back_pre) * slope_ref[0]).astype(BF16)
    grad_in = dot_nt(bessel_ref[...], back_pre)
    back_bessel = dot_nn(w_in_ref[...].astype(BF16), back_pre)

    back_dist = jnp.sum(back_bessel * slope_b_ref[...], axis=0, keepdims=True)
    x, y, z, inverse = (geo_ref[n : n + 1, :] for n in range(4))
    g = [None] + [harm_back_ref[k : k + 1, :] for k in range(1, harm_count)]
    xx, yy, zz = x * x, y * y, z * z
    five = CUBIC_C * (5.0 * zz - 1.0)
    three = 3.0 * CUBIC_A * (xx - yy)
    cross = 6.0 * CUBIC_A * x * y
    along_x = (
        SQRT3 * g[1]
        + SQRT15 * (y * g[4] + z * g[7] + x * g[8])
        + cross * g[9]
        + CUBIC_B * (y * z * g[10] + z * x * g[14])
        + five * g[13]
        + three * g[15]
    )
    along_y = (
        SQRT3 * g[2]
        + SQRT15 * (x * g[4] + z * g[5] - y * g[8])
        + three * g[9]
        + CUBIC_B * (x * z * g[10] - z * y * g[14])
        + five * g[11]
        - cross * g[15]
    )
    along_z = (
        SQRT3 * g[3]
        + SQRT15 * (y * g[5] + x * g[7])
        + 3.0 * SQRT5 * z * g[6]
        + CUBIC_B * (x * y * g[10] + 0.5 * (xx - yy) * g[14])
        + 10.0 * CUBIC_C * z * (y * g[11] + x * g[13])
        + 1.5 * SQRT7 * (5.0 * zz - 1.0) * g[12]
    )
    inward = back_dist - inverse * (x * along_x + y * along_y + z * along_z)
    back_relative = jnp.concatenate(
        [
            inverse * along_x + x * inward,
            inverse * along_y + y * inward,
            inverse * along_z + z * inward,
            jnp.zeros((BACK_ROWS - channels - 3, slots), F32),
        ],
        axis=0,
    )
    high, rest = halves(back_relative)
    stack_ref[channels:BACK_ROWS, :] = high
    stack_ref[BACK_ROWS + channels :, :] = rest
    spread = dot_nt(stack_ref[...], source_hot_ref[...])
    spread = spread[:BACK_ROWS, :] + spread[BACK_ROWS:, :]
    target_back = dot_nt(jnp.concatenate([high, rest], axis=0), target_hot_ref[...])
    size = BACK_ROWS - channels
    target_back = target_back[:size, :] + target_back[size:, :]
    owned_ref[0:channels, :] = spread[:channels, :atoms] + back_local
    owned_ref[channels:, :] = spread[channels:, :atoms] - target_back
    face = 0
    for ref in face_out:
        for part in range(ref.shape[0] // BACK_ROWS):
            start = atoms + face * LANES
            ref[part * BACK_ROWS : (part + 1) * BACK_ROWS, :] = spread[:, start : start + LANES]
            face += 1

    pack_ref[0:64, :] = grad_out[:, :LANES]
    pack_ref[64:128, :] = grad_out[:, LANES:]
    pack_ref[128:192, :] = jnp.concatenate([grad_degree[0], grad_degree[1]], axis=1)
    pack_ref[192:256, :] = jnp.concatenate([grad_degree[2], grad_degree[3]], axis=1)
    pack_ref[256:320, :] = jnp.concatenate([grad_species[0], grad_species[1]], axis=1)
    pack_ref[320:384, :] = jnp.concatenate([grad_species[2], grad_species[3]], axis=1)
    pack_ref[384:448, :] = jnp.concatenate([grad_hidden_one, grad_hidden_two], axis=1)
    pack_ref[448:456, :] = jnp.concatenate([grad_in, grad_readout], axis=1)
    if pack_ref.shape[0] > PACK_ROWS:
        pack_ref[PACK_ROWS:, :] = jnp.zeros((pack_ref.shape[0] - PACK_ROWS, LANES), F32)


def collect_kernel(face_count, parts_ref, owned_ref, halo_ref, *refs):
    face_in = refs[:face_count]
    share_ref, feature_ref, position_ref = refs[face_count:]
    channels, atoms = feature_ref.shape
    devices = parts_ref.shape[0]
    total = parts_ref[0].astype(F32)
    for n in range(1, devices):
        total += parts_ref[n].astype(F32)
    for n in range(devices):
        share_ref[n] = total
    pieces = []
    for ref in face_in:
        for part in range(ref.shape[0] // BACK_ROWS):
            pieces.append(ref[part * BACK_ROWS : (part + 1) * BACK_ROWS, :])
    returned = jnp.concatenate(pieces, axis=1)
    high, rest = halves(returned)
    halo = halo_ref[...]
    hot = jnp.concatenate(
        [one_hot(halo[face : face + 1, :], atoms) for face in range(halo.shape[0])], axis=1
    )
    added = dot_nt(jnp.concatenate([high, rest], axis=0), hot)
    owned = owned_ref[...] + added[:BACK_ROWS, :] + added[BACK_ROWS:, :]
    feature_ref[...] = owned[:channels, :]
    position_ref[...] = owned[channels : channels + 3, :]


def update_kernel(grad_ref, *refs):
    masters, moments, squares = refs[0:6], refs[6:12], refs[12:18]
    outs = refs[18:]

    def step(member, index, gradient):
        weight = masters[member][index]
        moment = BETA_ONE * moments[member][index] + (1.0 - BETA_ONE) * gradient
        square = BETA_TWO * squares[member][index] + (1.0 - BETA_TWO) * gradient * gradient
        corrected = (
            moment
            / (1.0 - BETA_ONE**STEP)
            / (jnp.sqrt(square / (1.0 - BETA_TWO**STEP)) + EPSILON)
        )
        outs[member][index] = weight - RATES[member] * (corrected + DECAY * weight)
        outs[6 + member][index] = moment
        outs[12 + member][index] = square

    step(0, Ellipsis, grad_ref[448:456, :64])
    step(1, 0, grad_ref[384:448, :64])
    step(1, 1, grad_ref[384:448, 64:])
    step(2, (slice(None), slice(0, LANES)), grad_ref[0:64, :])
    step(2, (slice(None), slice(LANES, 2 * LANES)), grad_ref[64:128, :])
    for base, member in ((128, 3), (256, 4)):
        for n in range(4):
            first = base + 64 * (n // 2)
            half = 64 * (n % 2)
            step(member, n, grad_ref[first : first + 64, half : half + 64])
    step(5, Ellipsis, grad_ref[448:450, 64:])


def shifted(value, axis, steps):
    count = lax.axis_size(axis)
    pairs = [(source, (source + steps) % count) for source in range(count)]
    return lax.ppermute(value, axis, pairs)


def vmem(count):
    return [pl.BlockSpec(memory_space=pltpu.VMEM)] * count


def shape(dims, dtype=F32):
    return jax.ShapeDtypeStruct(dims, dtype)


def on_device(*arguments):
    (
        node_feats,
        edge_vectors,
        edge_source,
        edge_target,
        edge_count,
        halo_index,
        atom_species,
        site_cotangent,
    ) = arguments[:8]
    masters, moments, squares = arguments[8:14], arguments[14:20], arguments[20:26]
    radial_input, radial_hidden, radial_output, degree_mix, species_mix, readout_weights = masters
    channels, atoms = node_feats.shape
    slots = edge_vectors.shape[1]
    width = halo_index.shape[1]
    extended = atoms + 6 * width
    devices = lax.axis_size(AXES)
    scale = 1.0 / max(1, 5 * slots // (8 * atoms))
    share = -(-PACK_ROWS // devices)
    share = -(-share // 8) * 8
    params = pltpu.CompilerParams(vmem_limit_bytes=VMEM_LIMIT)
    smem = [pl.BlockSpec(memory_space=pltpu.SMEM)]

    routes = []
    for axis in AXES:
        if lax.axis_size(axis) == 2:
            routes.append((axis, 1, 2))
        else:
            routes.append((axis, 1, 1))
            routes.append((axis, -1, 1))

    source = edge_source.reshape(slots // LANES, LANES)
    target = edge_target.reshape(slots // LANES, LANES)
    species = atom_species.reshape(atoms // LANES, LANES)
    cotangent = site_cotangent.reshape(atoms // LANES, LANES)

    faces = pl.pallas_call(
        pick_faces_kernel,
        out_shape=[shape((parts * channels, width), BF16) for _, _, parts in routes],
        in_specs=vmem(2),
        out_specs=vmem(len(routes)),
        compiler_params=params,
        name="pick_faces",
    )(node_feats, halo_index)
    arrived = [shifted(face, axis, way) for face, (axis, way, _) in zip(faces, routes)]

    edge_parts = pl.pallas_call(
        radial_kernel,
        out_shape=[
            shape((channels, slots), BF16),
            shape((16, slots)),
            shape((4, slots)),
            shape((NBASIS, slots)),
            shape((NBASIS, slots), BF16),
            shape((3, channels, slots), BF16),
            shape((3, channels, slots)),
            shape((4 * channels, slots)),
            shape((channels, atoms)),
        ],
        in_specs=smem + vmem(8),
        out_specs=vmem(9),
        compiler_params=params,
        name="radial",
        cost_estimate=pl.CostEstimate(
            flops=2 * slots * 64 * 1024, bytes_accessed=8 << 20, transcendentals=0
        ),
    )(
        edge_count,
        node_feats,
        edge_vectors,
        source,
        species,
        radial_input,
        radial_hidden,
        radial_output,
        species_mix,
    )

    results = pl.pallas_call(
        lambda *refs: layer_kernel(scale, len(routes), *refs),
        out_shape=[
            shape((1, atoms)),
            shape((BACK_ROWS, atoms)),
            shape((share * devices, LANES)),
        ]
        + [shape((parts * BACK_ROWS, width)) for _, _, parts in routes],
        in_specs=smem + vmem(len(routes) + 20),
        out_specs=vmem(3 + len(routes)),
        scratch_shapes=[
            pltpu.VMEM((channels, slots), F32),
            pltpu.VMEM((16 * channels, 2 * TILE), BF16),
            pltpu.VMEM((16 * channels, atoms), F32),
            pltpu.VMEM((16 * channels, atoms), BF16),
            pltpu.VMEM((16 * channels, atoms), BF16),
            pltpu.VMEM((4 * channels, slots), F32),
            pltpu.VMEM((4 * channels, slots), F32),
            pltpu.VMEM((16, slots), F32),
            pltpu.VMEM((4 * channels, slots), BF16),
            pltpu.VMEM((2 * BACK_ROWS, slots), BF16),
            pltpu.VMEM((atoms, slots), BF16),
            pltpu.VMEM((extended, slots), BF16),
        ],
        compiler_params=params,
        name="layer",
    )(
        edge_count,
        *arrived,
        *edge_parts,
        node_feats,
        source,
        target,
        species,
        cotangent,
        radial_input,
        radial_hidden,
        radial_output,
        degree_mix,
        species_mix,
        readout_weights,
    )
    energy, owned, packed = results[:3]
    returned = [
        shifted(back, axis, -way) for back, (axis, way, _) in zip(results[3:], routes)
    ]
    parts = lax.all_to_all(packed.reshape(devices, share, LANES), AXES, 0, 0, tiled=True)
    shares, feature_grad, position_grad = pl.pallas_call(
        lambda *refs: collect_kernel(len(routes), *refs),
        out_shape=[
            shape((devices, share, LANES)),
            shape((channels, atoms)),
            shape((3, atoms)),
        ],
        in_specs=vmem(3 + len(routes)),
        out_specs=vmem(3),
        compiler_params=params,
        name="collect",
    )(parts, owned, halo_index, *returned)
    gradient = lax.all_to_all(shares, AXES, 0, 0, tiled=True).reshape(devices * share, LANES)
    updated = pl.pallas_call(
        update_kernel,
        out_shape=[shape(member.shape) for member in masters + masters + masters],
        in_specs=vmem(19),
        out_specs=vmem(18),
        compiler_params=params,
        name="update",
    )(gradient, *masters, *moments, *squares)
    return (energy.reshape(atoms), feature_grad, position_grad, *updated)


def solution(mesh):
    split = P(AXES)
    split_last = P(None, AXES)
    in_specs = (
        split_last,
        split_last,
        split,
        split,
        split,
        split_last,
        split,
        split,
    ) + (P(),) * 18
    out_specs = (split, split_last, split_last) + (P(),) * 18
    return jax.shard_map(
        on_device, mesh=mesh, in_specs=in_specs, out_specs=out_specs, check_vma=False
    )
```

time: 742 us -> 75.8 us (0.10); the launches traced: 733 us -> 75 us
  other arithmetic: 459 us -> 0 us
  local copies, waits for them, and re-layouts: 113 us -> 15.8 us
  waiting for transfers between devices: 68 us -> 5.83 us
  blocking collectives: 39.8 us -> 12 us
  Pallas kernels: 0 us -> 21.7 us
  matrix products: 20.8 us -> 0 us
  between operations: 16 us -> 1.8 us
    scatter-add x10 -> x0, other arithmetic: 294 us -> none  [the longest x1 248 us: on_device(): jnp.zeros((16, channels, local_atoms), jnp.float32).at[:, :, edge_target]]
    reduce_sum x8 -> x0, other arithmetic: 111 us -> none  [the longest x1 66.2 us: on_device(): back_harmonic = jnp.sum(weighted_back * spread, axis=1)]
    psum x1 -> x0, waiting for transfers between devices: 68 us -> none  [on_device(): lax.psum((grads[0], grads[1], grads[2], grads[3], grads[4], grads[5]), ('...]
    psum x1 -> x0, blocking collectives: 39.8 us -> none  [on_device(): lax.psum((grads[0], grads[1], grads[2], grads[3], grads[4], grads[5]), ('...]
    gather x8 -> x0, local copies, waits for them, and re-layouts: 31.5 us -> none  [the longest x1 21.1 us: on_device(): back_message = jnp.take(back_summed, edge_target, axis=2) * inverse_avg]
    pallas_call x0 -> x5, Pallas kernels: none -> 21.7 us  [the longest x1 16.3 us: on_device(): pl.pallas_call(lambda *refs: layer_kernel(scale, len(routes), *refs), out...]
    dot_general x27 -> x0, matrix products: 20.8 us -> none  [the longest x4 5.22 us: outer_sum(): jnp.einsum('fe,ke->fk', left, right, preferred_element_type=jnp.float32)]
    unnamed x168 -> x78, local copies, waits for them, and re-layouts: 34.2 us -> 15.8 us
  transfers between devices with their start and end apart: 13 -> 11, of which waited for: 1 -> 3; matrix products, arithmetic and copies ran while one was open for 8% -> 0% of each run, Pallas kernels for 0% -> 4%
where the time goes in v1:
time: 75.8 us; the launch traced here: 75 us
  Pallas kernels  21.7 us (29%)
  starting transfers between devices  17.8 us (23%)
  local copies, waits for them, and re-layouts  15.8 us (21%)
  blocking collectives  12 us (16%)
  waiting for transfers between devices  5.83 us (8%)
  between operations  1.8 us (2%)
    pallas_call x1, Pallas kernels, on_device(): pl.pallas_call(lambda *refs: layer_kernel(scale, len(routes), *refs), out...  16.3 us
    unnamed x78, local copies, waits for them, and re-layouts  15.8 us
    ppermute x10, starting transfers between devices, shifted(): return lax.ppermute(value, axis, pairs)  14.7 us
    all_to_all x1, blocking collectives, on_device(): lax.all_to_all(shares, AXES, 0, 0, tiled=True)  12 us
    ppermute x10, waiting for transfers between devices, shifted(): return lax.ppermute(value, axis, pairs)  5.83 us
    all_to_all x1, starting transfers between devices, on_device(): lax.all_to_all(packed.reshape(devices, share, LANES), AXES, 0, 0, tiled=T...  3.12 us
    pallas_call x1, Pallas kernels, on_device(): pl.pallas_call(radial_kernel, out_shape=[shape((channels, slots), BF16),...  2.81 us
  transfers between devices with their start and end apart: 11, of which 3 were waited for; matrix products, arithmetic and copies ran while one was open for 0% of the time, Pallas kernels for 4%

profile of v1, /device:TPU:0, one launch (start us, length us, event | category | flops | bytes accessed | tf_op | source)
XLA Modules:
  0.0 75.0 jit_solution(5797736157072834507)
XLA Ops:
  0.7 0.8 %copy-done.12 = bf16[64,512]{1,0:T(8,128)(2,1)S(1)} copy-done((bf16[64,512]{1,0:T(8,128)(2,1)S(1)}, bf16[64,512]{1,0:T(8,128)(2,1)}, u32[]{:S(2)}) %copy-start.12) | copy-done | bytes 65560
  1.5 0.7 copy-done.24
  2.2 0.3 pick_faces.1
  2.5 3.0 %collective-permute-start = (bf16[128,128]{1,0:T(8,128)(2,1)S(1)}, bf16[128,128]{1,0:T(8,128)(2,1)S(1)}, u32[]{:S(2)}, u32[]{:S(2)}) collective-permute-start(bf16[128,128]{1,0:T(8,128)(2,1)S(1)} %get-tuple-element.64), channel_id=1, source_target_pairs={{0,16},{16,0},{1,17},{17,1},{2,18},{18,2},{3,19},{19,3},{4,20},{20... | collective-permute-start | bytes 98312 | tf_op jit(solution)/shard_map/ppermute | solution.py:513
  5.5 1.7 %collective-permute-start.2 = (bf16[64,128]{1,0:T(8,128)(2,1)S(1)}, bf16[64,128]{1,0:T(8,128)(2,1)S(1)}, u32[]{:S(2)}, u32[]{:S(2)}) collective-permute-start(bf16[64,128]{1,0:T(8,128)(2,1)S(1)} %get-tuple-element.66), channel_id=1, source_target_pairs={{0,12},{4,0},{8,4},{12,8},{1,13},{5,1},{9,5},{13,9},{2,14},{6,2},{... | collective-permute-start | bytes 49160 | tf_op jit(solution)/shard_map/ppermute | solution.py:513
  7.2 1.6 %collective-permute-start.3 = (bf16[64,128]{1,0:T(8,128)(2,1)S(1)}, bf16[64,128]{1,0:T(8,128)(2,1)S(1)}, u32[]{:S(2)}, u32[]{:S(2)}) collective-permute-start(bf16[64,128]{1,0:T(8,128)(2,1)S(1)} %get-tuple-element.67), channel_id=1, source_target_pairs={{0,1},{1,2},{2,3},{3,0},{4,5},{5,6},{6,7},{7,4},{8,9},{9,10},{10,1... | collective-permute-start | bytes 49160 | tf_op jit(solution)/shard_map/ppermute | solution.py:513
  8.8 2.2 %collective-permute-start.4 = (bf16[64,128]{1,0:T(8,128)(2,1)S(1)}, bf16[64,128]{1,0:T(8,128)(2,1)S(1)}, u32[]{:S(2)}, u32[]{:S(2)}) collective-permute-start(bf16[64,128]{1,0:T(8,128)(2,1)S(1)} %get-tuple-element.68), channel_id=1, source_target_pairs={{0,3},{1,0},{2,1},{3,2},{4,7},{5,4},{6,5},{7,6},{8,11},{9,8},{10,9... | collective-permute-start | bytes 49160 | tf_op jit(solution)/shard_map/ppermute | solution.py:513
  11.7 0.0 copy-start.1
  11.7 0.9 %copy-done.1 = f32[4,64,64]{2,1,0:T(8,128)S(1)} copy-done((f32[4,64,64]{2,1,0:T(8,128)S(1)}, f32[4,64,64]{2,1,0:T(8,128)}, u32[]{:S(2)}) %copy-start.1) | copy-done | bytes 65560
  12.6 0.8 %copy-done.6 = f32[2,64,64]{2,1,0:T(8,128)S(1)} copy-done((f32[2,64,64]{2,1,0:T(8,128)S(1)}, f32[2,64,64]{2,1,0:T(8,128)}, u32[]{:S(2)}) %copy-start.6) | copy-done | bytes 32792
  13.4 0.8 %copy-done.9 = f32[64,256]{1,0:T(8,128)S(1)} copy-done((f32[64,256]{1,0:T(8,128)S(1)}, f32[64,256]{1,0:T(8,128)}, u32[]{:S(2)}) %copy-start.9) | copy-done | bytes 65560
  14.3 0.7 copy-done.21
  15.0 0.7 copy-done.26
  15.7 0.7 copy-done.33
  16.3 0.8 %copy-done.38 = f32[3,2048]{1,0:T(4,128)S(1)} copy-done((f32[3,2048]{1,0:T(4,128)S(1)}, f32[3,2048]{1,0:T(4,128)}, u32[]{:S(2)}) %copy-start.38) | copy-done | bytes 24600
  17.1 2.8 %radial.1 = (bf16[64,2048]{1,0:T(8,128)(2,1)S(1)}, f32[16,2048]{1,0:T(8,128)S(1)}, f32[4,2048]{1,0:T(4,128)S(1)}, f32[8,2048]{1,0:T(8,128)S(1)}, bf16[8,2048]{1,...) custom-call(s32[1]{0:T(128)S(6)} %copy.47.count_ref.refs_0_, ...), custom_call_target="tpu_custom_call" | custom-call | flops 268435456 | bytes 8388608 | tf_op jit(solution)/shard_map/radial/pallas_call | solution.py:571
  19.9 1.1 %copy-done = f32[3,64,2048]{2,1,0:T(8,128)} copy-done((f32[3,64,2048]{2,1,0:T(8,128)}, f32[3,64,2048]{2,1,0:T(8,128)S(1)}, u32[]{:S(2)}) %copy-start) | copy-done | bytes 1572888
  21.1 0.0 copy-start.2
  21.1 0.9 %copy-done.2 = f32[4,64,64]{2,1,0:T(8,128)S(1)} copy-done((f32[4,64,64]{2,1,0:T(8,128)S(1)}, f32[4,64,64]{2,1,0:T(8,128)}, u32[]{:S(2)}) %copy-start.2) | copy-done | bytes 65560
  22.0 0.9 %copy-done.4 = f32[4,64,64]{2,1,0:T(8,128)S(1)} copy-done((f32[4,64,64]{2,1,0:T(8,128)S(1)}, f32[4,64,64]{2,1,0:T(8,128)}, u32[]{:S(2)}) %copy-start.4) | copy-done | bytes 65560
  22.9 0.8 %copy-done.7 = f32[2,64,64]{2,1,0:T(8,128)S(1)} copy-done((f32[2,64,64]{2,1,0:T(8,128)S(1)}, f32[2,64,64]{2,1,0:T(8,128)}, u32[]{:S(2)}) %copy-start.7) | copy-done | bytes 32792
  23.7 0.8 %copy-done.10 = f32[64,256]{1,0:T(8,128)S(1)} copy-done((f32[64,256]{1,0:T(8,128)S(1)}, f32[64,256]{1,0:T(8,128)}, u32[]{:S(2)}) %copy-start.10) | copy-done | bytes 65560
  24.6 0.7 copy-done.22
  25.3 0.7 copy-done.27
  26.0 0.7 copy-done.28
  26.7 0.7 copy-done.31
  27.3 0.7 copy-done.34
  28.0 0.7 copy-done.35
  28.7 0.0 copy-start.13
  28.7 0.0 copy-start.14
  28.7 0.0 copy-start.15
  28.8 0.0 copy-start.16
  28.8 0.0 copy-start.17
  28.8 0.0 copy-start.18
  28.8 0.0 copy-start.19
  28.8 0.0 copy-start.30
  28.9 0.0 copy-start.36
  28.9 16.3 %layer.1 = (f32[1,512]{1,0:T(1,128)}, f32[80,512]{1,0:T(8,128)S(1)}, f32[512,128]{1,0:T(8,128)}, f32[160,128]{1,0:T(8,128)S(1)}, f32[80,128]{1,0:T(8,128)S(1)}, ...) custom-call(s32[1]{0:T(128)S(6)} %copy.47.count_ref.refs_0_, ...), custom_call_target="tpu_custom_call" | custom-call | tf_op jit(solution)/shard_map/layer/pallas_call | solution.py:603
  45.2 3.1 %all-to-all-start = ((f32[32,16,128]{2,1,0:T(8,128)}), f32[32,16,128]{2,1,0:T(8,128)S(1)}, u32[]{:S(2)}, u32[]{:S(2)}) async-start(f32[32,16,128]{2,1,0:T(8,128)} %bitcast.5), calls=%async_computation | async-start | bytes 524288 | tf_op jit(solution)/shard_map/all_to_all | solution.py:649
  48.3 1.8 %collective-permute-start.5 = (f32[160,128]{1,0:T(8,128)S(1)}, f32[160,128]{1,0:T(8,128)S(1)}, u32[]{:S(2)}, u32[]{:S(2)}) collective-permute-start(f32[160,128]{1,0:T(8,128)S(1)} %get-tuple-element.81), channel_id=1, source_target_pairs={{0,16},{16,0},{1,17},{17,1},{2,18},{18,2},{3,19},{19,3},{4,20},{20... | collective-permute-start | bytes 245768 | tf_op jit(solution)/shard_map/ppermute | solution.py:513
  50.1 0.9 %collective-permute-start.6 = (f32[80,128]{1,0:T(8,128)S(1)}, f32[80,128]{1,0:T(8,128)S(1)}, u32[]{:S(2)}, u32[]{:S(2)}) collective-permute-start(f32[80,128]{1,0:T(8,128)S(1)} %get-tuple-element.82), channel_id=1, source_target_pairs={{0,12},{4,0},{8,4},{12,8},{1,13},{5,1},{9,5},{13,9},{2,14},{6,2},{... | collective-permute-start | bytes 122888 | tf_op jit(solution)/shard_map/ppermute | solution.py:513
  51.1 3.4 %collective-permute-start.8 = (f32[80,128]{1,0:T(8,128)S(1)}, f32[80,128]{1,0:T(8,128)S(1)}, u32[]{:S(2)}, u32[]{:S(2)}) collective-permute-start(f32[80,128]{1,0:T(8,128)S(1)} %get-tuple-element.84), channel_id=1, source_target_pairs={{0,3},{1,0},{2,1},{3,2},{4,7},{5,4},{6,5},{7,6},{8,11},{9,8},{10,9... | collective-permute-start | bytes 122888 | tf_op jit(solution)/shard_map/ppermute | solution.py:513
  54.4 0.3 collective-permute-done.7.refs_5_
  54.7 1.6 %collective-permute-done.8.refs_6_ = f32[80,128]{1,0:T(8,128)S(1)} collective-permute-done((f32[80,128]{1,0:T(8,128)S(1)}, f32[80,128]{1,0:T(8,128)S(1)}, u32[]{:S(2)}, u32[]{:S(2)}) %collective-permute-start.8) | collective-permute-done | bytes 40992 | tf_op jit(solution)/shard_map/ppermute | solution.py:513
  56.4 3.9 %collective-permute-done.9.refs_7_ = f32[80,128]{1,0:T(8,128)S(1)} collective-permute-done((f32[80,128]{1,0:T(8,128)S(1)}, f32[80,128]{1,0:T(8,128)S(1)}, u32[]{:S(2)}, u32[]{:S(2)}) %collective-permute-start.9) | collective-permute-done | bytes 40992 | tf_op jit(solution)/shard_map/ppermute | solution.py:513
  60.3 1.1 %collect.1 = (f32[32,16,128]{2,1,0:T(8,128)S(1)}, f32[64,512]{1,0:T(8,128)}, f32[3,512]{1,0:T(4,128)}) custom-call(f32[32,16,128]{2,1,0:T(8,128)S(1)} %all-to-all-done.refs_0_, f32[80,512]{1,0:T(8,128)S(1)} %get-tuple-element.80.refs_1_, s32[6,128]{1,0:T(8,128)S(1)} %copy-done.25, f32[160,128]{1,0:T(8,128)S(1)} %collective-permute-done.5.refs_3_, ...), custom_call_target="tpu_custom_call" | custom-call | tf_op jit(solution)/shard_map/collect/pallas_call | solution.py:650
  61.3 12.0 %all_to_all.10 = f32[32,16,128]{2,1,0:T(8,128)S(1)} all-to-all(f32[32,16,128]{2,1,0:T(8,128)S(1)} %get-tuple-element.88), channel_id=1, replica_groups=mesh['gx'=2,'gy'=4,'gz'=4] {'gx','gy','gz'}, dimensions={0} | all-to-all | bytes 524288 | tf_op jit(solution)/shard_map/all_to_all | solution.py:662
  73.5 1.3 %update.1 = (f32[8,64]{1,0:T(8,128)}, f32[2,64,64]{2,1,0:T(8,128)}, f32[64,256]{1,0:T(8,128)}, f32[4,64,64]{2,1,0:T(8,128)}, f32[4,64,64]{2,1,0:T(8,128)}, /*ind...) custom-call(f32[512,128]{1,0:T(8,128)S(1)} %bitcast.7, ...), custom_call_target="tpu_custom_call" | custom-call | tf_op jit(solution)/shard_map/update/pallas_call | solution.py:663
  (58 shorter events, 0.1 us)
Async XLA Ops:
  0.7 0.8 %copy-start.12 = (bf16[64,512]{1,0:T(8,128)(2,1)S(1)}, bf16[64,512]{1,0:T(8,128)(2,1)}, u32[]{:S(2)}) copy-start(bf16[64,512]{1,0:T(8,128)(2,1)} %refs_15_.2) | copy-start | bytes 196612
  1.5 0.7 copy-start.24
  2.5 18.6 %collective-permute-start = (bf16[128,128]{1,0:T(8,128)(2,1)S(1)}, bf16[128,128]{1,0:T(8,128)(2,1)S(1)}, u32[]{:S(2)}, u32[]{:S(2)}) collective-permute-start(bf16[128,128]{1,0:T(8,128)(2,1)S(1)} %get-tuple-element.64), channel_id=1, source_target_pairs={{0,16},{16,0},{1,17},{17,1},{2,18},{18,2},{3,19},{19,3},{4,20},{20... | collective-permute-start | bytes 98312 | tf_op jit(solution)/shard_map/ppermute | solution.py:513
  5.5 15.6 %collective-permute-start.1 = (bf16[64,128]{1,0:T(8,128)(2,1)S(1)}, bf16[64,128]{1,0:T(8,128)(2,1)S(1)}, u32[]{:S(2)}, u32[]{:S(2)}) collective-permute-start(bf16[64,128]{1,0:T(8,128)(2,1)S(1)} %get-tuple-element.65), channel_id=1, source_target_pairs={{0,4},{4,8},{8,12},{12,0},{1,5},{5,9},{9,13},{13,1},{2,6},{6,10},{... | collective-permute-start | bytes 49160 | tf_op jit(solution)/shard_map/ppermute | solution.py:513
  5.5 15.6 %collective-permute-start.2 = (bf16[64,128]{1,0:T(8,128)(2,1)S(1)}, bf16[64,128]{1,0:T(8,128)(2,1)S(1)}, u32[]{:S(2)}, u32[]{:S(2)}) collective-permute-start(bf16[64,128]{1,0:T(8,128)(2,1)S(1)} %get-tuple-element.66), channel_id=1, source_target_pairs={{0,12},{4,0},{8,4},{12,8},{1,13},{5,1},{9,5},{13,9},{2,14},{6,2},{... | collective-permute-start | bytes 49160 | tf_op jit(solution)/shard_map/ppermute | solution.py:513
  7.2 13.9 %collective-permute-start.3 = (bf16[64,128]{1,0:T(8,128)(2,1)S(1)}, bf16[64,128]{1,0:T(8,128)(2,1)S(1)}, u32[]{:S(2)}, u32[]{:S(2)}) collective-permute-start(bf16[64,128]{1,0:T(8,128)(2,1)S(1)} %get-tuple-element.67), channel_id=1, source_target_pairs={{0,1},{1,2},{2,3},{3,0},{4,5},{5,6},{6,7},{7,4},{8,9},{9,10},{10,1... | collective-permute-start | bytes 49160 | tf_op jit(solution)/shard_map/ppermute | solution.py:513
  8.8 12.3 %collective-permute-start.4 = (bf16[64,128]{1,0:T(8,128)(2,1)S(1)}, bf16[64,128]{1,0:T(8,128)(2,1)S(1)}, u32[]{:S(2)}, u32[]{:S(2)}) collective-permute-start(bf16[64,128]{1,0:T(8,128)(2,1)S(1)} %get-tuple-element.68), channel_id=1, source_target_pairs={{0,3},{1,0},{2,1},{3,2},{4,7},{5,4},{6,5},{7,6},{8,11},{9,8},{10,9... | collective-permute-start | bytes 49160 | tf_op jit(solution)/shard_map/ppermute | solution.py:513
  11.7 0.9 %copy-start.1 = (f32[4,64,64]{2,1,0:T(8,128)S(1)}, f32[4,64,64]{2,1,0:T(8,128)}, u32[]{:S(2)}) copy-start(f32[4,64,64]{2,1,0:T(8,128)} %refs_4_.1) | copy-start | bytes 196612
  12.6 0.8 %copy-start.6 = (f32[2,64,64]{2,1,0:T(8,128)S(1)}, f32[2,64,64]{2,1,0:T(8,128)}, u32[]{:S(2)}) copy-start(f32[2,64,64]{2,1,0:T(8,128)} %refs_1_.1) | copy-start | bytes 98308
  13.4 0.8 %copy-start.9 = (f32[64,256]{1,0:T(8,128)S(1)}, f32[64,256]{1,0:T(8,128)}, u32[]{:S(2)}) copy-start(f32[64,256]{1,0:T(8,128)} %refs_2_.3) | copy-start | bytes 196612
  14.3 0.7 copy-start.21
  15.0 0.7 copy-start.26
  15.7 0.7 copy-start.33
  16.3 0.8 %copy-start.38 = (f32[3,2048]{1,0:T(4,128)S(1)}, f32[3,2048]{1,0:T(4,128)}, u32[]{:S(2)}) copy-start(f32[3,2048]{1,0:T(4,128)} %vectors_ref.1) | copy-start | bytes 73732
  19.9 1.1 %copy-start = (f32[3,64,2048]{2,1,0:T(8,128)}, f32[3,64,2048]{2,1,0:T(8,128)S(1)}, u32[]{:S(2)}) copy-start(f32[3,64,2048]{2,1,0:T(8,128)S(1)} %get-tuple-element.75.refs_12_) | copy-start | bytes 4718596
  21.1 0.9 %copy-start.2 = (f32[4,64,64]{2,1,0:T(8,128)S(1)}, f32[4,64,64]{2,1,0:T(8,128)}, u32[]{:S(2)}) copy-start(f32[4,64,64]{2,1,0:T(8,128)} %refs_4_.1) | copy-start | bytes 196612
  22.0 0.9 %copy-start.4 = (f32[4,64,64]{2,1,0:T(8,128)S(1)}, f32[4,64,64]{2,1,0:T(8,128)}, u32[]{:S(2)}) copy-start(f32[4,64,64]{2,1,0:T(8,128)} %refs_3_.1) | copy-start | bytes 196612
  22.9 0.8 %copy-start.7 = (f32[2,64,64]{2,1,0:T(8,128)S(1)}, f32[2,64,64]{2,1,0:T(8,128)}, u32[]{:S(2)}) copy-start(f32[2,64,64]{2,1,0:T(8,128)} %refs_1_.1) | copy-start | bytes 98308
  23.7 0.8 %copy-start.10 = (f32[64,256]{1,0:T(8,128)S(1)}, f32[64,256]{1,0:T(8,128)}, u32[]{:S(2)}) copy-start(f32[64,256]{1,0:T(8,128)} %refs_2_.3) | copy-start | bytes 196612
  24.6 0.7 copy-start.22
  25.3 0.7 copy-start.27
  26.0 0.7 copy-start.28
  27.3 0.7 copy-start.34
  28.7 31.6 %copy-start.25 = (s32[6,128]{1,0:T(8,128)S(1)}, s32[6,128]{1,0:T(8,128)}, u32[]{:S(2)}) copy-start(s32[6,128]{1,0:T(8,128)} %refs_2_.2) | copy-start | bytes 9220
  28.7 44.6 %copy-start.3 = (f32[4,64,64]{2,1,0:T(8,128)S(1)}, f32[4,64,64]{2,1,0:T(8,128)}, u32[]{:S(2)}) copy-start(f32[4,64,64]{2,1,0:T(8,128)} %refs_4_.1) | copy-start | bytes 196612
  28.7 44.6 %copy-start.5 = (f32[4,64,64]{2,1,0:T(8,128)S(1)}, f32[4,64,64]{2,1,0:T(8,128)}, u32[]{:S(2)}) copy-start(f32[4,64,64]{2,1,0:T(8,128)} %refs_3_.1) | copy-start | bytes 196612
  28.7 44.6 %copy-start.8 = (f32[2,64,64]{2,1,0:T(8,128)S(1)}, f32[2,64,64]{2,1,0:T(8,128)}, u32[]{:S(2)}) copy-start(f32[2,64,64]{2,1,0:T(8,128)} %refs_1_.1) | copy-start | bytes 98308
  28.7 44.6 %copy-start.11 = (f32[64,256]{1,0:T(8,128)S(1)}, f32[64,256]{1,0:T(8,128)}, u32[]{:S(2)}) copy-start(f32[64,256]{1,0:T(8,128)} %refs_2_.3) | copy-start | bytes 196612
  28.7 44.6 %copy-start.13 = (f32[4,64,64]{2,1,0:T(8,128)S(1)}, f32[4,64,64]{2,1,0:T(8,128)}, u32[]{:S(2)}) copy-start(f32[4,64,64]{2,1,0:T(8,128)} %refs_9_.1) | copy-start | bytes 196612
  28.7 44.6 %copy-start.14 = (f32[4,64,64]{2,1,0:T(8,128)S(1)}, f32[4,64,64]{2,1,0:T(8,128)}, u32[]{:S(2)}) copy-start(f32[4,64,64]{2,1,0:T(8,128)} %refs_10_.1) | copy-start | bytes 196612
  28.7 44.6 %copy-start.15 = (f32[4,64,64]{2,1,0:T(8,128)S(1)}, f32[4,64,64]{2,1,0:T(8,128)}, u32[]{:S(2)}) copy-start(f32[4,64,64]{2,1,0:T(8,128)} %refs_15_.3) | copy-start | bytes 196612
  28.8 44.6 %copy-start.16 = (f32[4,64,64]{2,1,0:T(8,128)S(1)}, f32[4,64,64]{2,1,0:T(8,128)}, u32[]{:S(2)}) copy-start(f32[4,64,64]{2,1,0:T(8,128)} %refs_16_.1) | copy-start | bytes 196612
  28.8 44.6 %copy-start.17 = (f32[2,64,64]{2,1,0:T(8,128)S(1)}, f32[2,64,64]{2,1,0:T(8,128)}, u32[]{:S(2)}) copy-start(f32[2,64,64]{2,1,0:T(8,128)} %refs_7_.1) | copy-start | bytes 98308
  28.8 44.6 %copy-start.18 = (f32[64,256]{1,0:T(8,128)S(1)}, f32[64,256]{1,0:T(8,128)}, u32[]{:S(2)}) copy-start(f32[64,256]{1,0:T(8,128)} %refs_8_.1) | copy-start | bytes 196612
  28.8 44.6 %copy-start.19 = (f32[2,64,64]{2,1,0:T(8,128)S(1)}, f32[2,64,64]{2,1,0:T(8,128)}, u32[]{:S(2)}) copy-start(f32[2,64,64]{2,1,0:T(8,128)} %refs_13_.1) | copy-start | bytes 98308
  28.8 44.6 %copy-start.20 = (f32[64,256]{1,0:T(8,128)S(1)}, f32[64,256]{1,0:T(8,128)}, u32[]{:S(2)}) copy-start(f32[64,256]{1,0:T(8,128)} %refs_14_.1) | copy-start | bytes 196612
  28.8 44.6 %copy-start.23 = (f32[8,64]{1,0:T(8,128)S(1)}, f32[8,64]{1,0:T(8,128)}, u32[]{:S(2)}) copy-start(f32[8,64]{1,0:T(8,128)} %refs_0_.2) | copy-start | bytes 6148
  28.8 44.6 %copy-start.29 = (f32[8,64]{1,0:T(8,128)S(1)}, f32[8,64]{1,0:T(8,128)}, u32[]{:S(2)}) copy-start(f32[8,64]{1,0:T(8,128)} %refs_6_.1) | copy-start | bytes 6148
  28.8 44.6 %copy-start.30 = (f32[8,64]{1,0:T(8,128)S(1)}, f32[8,64]{1,0:T(8,128)}, u32[]{:S(2)}) copy-start(f32[8,64]{1,0:T(8,128)} %refs_12_.1) | copy-start | bytes 6148
  28.9 44.6 %copy-start.32 = (f32[2,64]{1,0:T(2,128)S(1)}, f32[2,64]{1,0:T(2,128)}, u32[]{:S(2)}) copy-start(f32[2,64]{1,0:T(2,128)} %refs_5_.1) | copy-start | bytes 1540
  28.9 44.6 %copy-start.36 = (f32[2,64]{1,0:T(2,128)S(1)}, f32[2,64]{1,0:T(2,128)}, u32[]{:S(2)}) copy-start(f32[2,64]{1,0:T(2,128)} %refs_11_.1) | copy-start | bytes 1540
  28.9 44.6 %copy-start.37 = (f32[2,64]{1,0:T(2,128)S(1)}, f32[2,64]{1,0:T(2,128)}, u32[]{:S(2)}) copy-start(f32[2,64]{1,0:T(2,128)} %refs_17_.1) | copy-start | bytes 1540
  45.2 15.1 %all-to-all-start = ((f32[32,16,128]{2,1,0:T(8,128)}), f32[32,16,128]{2,1,0:T(8,128)S(1)}, u32[]{:S(2)}, u32[]{:S(2)}) async-start(f32[32,16,128]{2,1,0:T(8,128)} %bitcast.5), calls=%async_computation | async-start | bytes 524288 | tf_op jit(solution)/shard_map/all_to_all | solution.py:649
  48.3 12.0 %collective-permute-start.5 = (f32[160,128]{1,0:T(8,128)S(1)}, f32[160,128]{1,0:T(8,128)S(1)}, u32[]{:S(2)}, u32[]{:S(2)}) collective-permute-start(f32[160,128]{1,0:T(8,128)S(1)} %get-tuple-element.81), channel_id=1, source_target_pairs={{0,16},{16,0},{1,17},{17,1},{2,18},{18,2},{3,19},{19,3},{4,20},{20... | collective-permute-start | bytes 245768 | tf_op jit(solution)/shard_map/ppermute | solution.py:513
  50.1 4.3 %collective-permute-start.6 = (f32[80,128]{1,0:T(8,128)S(1)}, f32[80,128]{1,0:T(8,128)S(1)}, u32[]{:S(2)}, u32[]{:S(2)}) collective-permute-start(f32[80,128]{1,0:T(8,128)S(1)} %get-tuple-element.82), channel_id=1, source_target_pairs={{0,12},{4,0},{8,4},{12,8},{1,13},{5,1},{9,5},{13,9},{2,14},{6,2},{... | collective-permute-start | bytes 122888 | tf_op jit(solution)/shard_map/ppermute | solution.py:513
  51.1 3.7 %collective-permute-start.7 = (f32[80,128]{1,0:T(8,128)S(1)}, f32[80,128]{1,0:T(8,128)S(1)}, u32[]{:S(2)}, u32[]{:S(2)}) collective-permute-start(f32[80,128]{1,0:T(8,128)S(1)} %get-tuple-element.83), channel_id=1, source_target_pairs={{0,4},{4,8},{8,12},{12,0},{1,5},{5,9},{9,13},{13,1},{2,6},{6,10},{... | collective-permute-start | bytes 122888 | tf_op jit(solution)/shard_map/ppermute | solution.py:513
  51.1 5.3 %collective-permute-start.8 = (f32[80,128]{1,0:T(8,128)S(1)}, f32[80,128]{1,0:T(8,128)S(1)}, u32[]{:S(2)}, u32[]{:S(2)}) collective-permute-start(f32[80,128]{1,0:T(8,128)S(1)} %get-tuple-element.84), channel_id=1, source_target_pairs={{0,3},{1,0},{2,1},{3,2},{4,7},{5,4},{6,5},{7,6},{8,11},{9,8},{10,9... | collective-permute-start | bytes 122888 | tf_op jit(solution)/shard_map/ppermute | solution.py:513
  54.4 5.8 %collective-permute-start.9 = (f32[80,128]{1,0:T(8,128)S(1)}, f32[80,128]{1,0:T(8,128)S(1)}, u32[]{:S(2)}, u32[]{:S(2)}) collective-permute-start(f32[80,128]{1,0:T(8,128)S(1)} %get-tuple-element.85), channel_id=1, source_target_pairs={{0,1},{1,2},{2,3},{3,0},{4,5},{5,6},{6,7},{7,4},{8,9},{9,10},{10,1... | collective-permute-start | bytes 122888 | tf_op jit(solution)/shard_map/ppermute | solution.py:513
  (2 other events, 1.4 us)

commit v2 on v1

--- a/solution.py
+++ b/solution.py
@@ -32,7 +32,7 @@
 TILE = 256
 BACK_ROWS = 80
 PACK_ROWS = 456
-VMEM_LIMIT = 50 * 1024 * 1024
+VMEM_LIMIT = 24 * 1024 * 1024
 
 
 def dot_nn(left, right):
@@ -88,8 +88,20 @@
     return jnp.sum(jnp.where(eye, column, 0.0), axis=0, keepdims=True)
 
 
-def pick_faces_kernel(feats_ref, halo_ref, *face_refs):
+def fetch(pairs, sems):
+    copies = [
+        pltpu.make_async_copy(source, place, sems.at[n]) for n, (source, place) in enumerate(pairs)
+    ]
+    for copy in copies:
+        copy.start()
+    return copies
+
+
+def pick_faces_kernel(feats_in, halo_in, feats_ref, *refs):
+    face_refs, (halo_ref, sems) = refs[:-2], refs[-2:]
     channels, atoms = feats_ref.shape
+    for copy in fetch([(feats_in, feats_ref), (halo_in, halo_ref)], sems):
+        copy.wait()
     feats = feats_ref[...]
     halo = halo_ref[...]
     face = 0
@@ -103,13 +115,17 @@
 def radial_kernel(
     count_ref,
     feats_ref,
-    vectors_ref,
-    source_ref,
-    species_ref,
-    w_in_ref,
-    w_hidden_ref,
-    w_out_ref,
-    w_species_ref,
+    vectors_in,
+    source_in,
+    target_in,
+    species_in,
+    cotangent_in,
+    w_in_in,
+    w_hidden_in,
+    w_out_in,
+    w_degree_in,
+    w_species_in,
+    readout_in,
     own_ref,
     harm_ref,
     geo_ref,
@@ -119,7 +135,41 @@
     slope_ref,
     radial_ref,
     self_ref,
+    source_ref,
+    target_ref,
+    species_ref,
+    cotangent_ref,
+    readout_ref,
+    w_in_ref,
+    w_hidden_ref,
+    w_out_ref,
+    w_degree_ref,
+    w_species_ref,
+    vectors_ref,
+    w_in_full,
+    w_hidden_full,
+    w_out_full,
+    w_degree_full,
+    w_species_full,
+    sems,
 ):
+    copies = fetch(
+        [
+            (vectors_in, vectors_ref),
+            (w_in_in, w_in_full),
+            (w_hidden_in, w_hidden_full),
+            (w_out_in, w_out_full),
+            (w_species_in, w_species_full),
+            (species_in, species_ref),
+            (source_in, source_ref),
+            (w_degree_in, w_degree_full),
+            (target_in, target_ref),
+            (cotangent_in, cotangent_ref),
+            (readout_in, readout_ref),
+        ],
+        sems,
+    )
+    copies[0].wait()
     channels, atoms = feats_ref.shape
     slots = vectors_ref.shape[1]
     vectors = vectors_ref[...]
@@ -166,17 +216,23 @@
     )
     geo_ref[0:3, :] = jnp.concatenate([x, y, z], axis=0)
     geo_ref[3:4, :] = inverse
-    w_in = w_in_ref[...].astype(BF16)
+    for copy in copies[1:]:
+        copy.wait()
+    w_in_ref[...] = w_in_full[...].astype(BF16)
+    w_hidden_ref[...] = w_hidden_full[...].astype(BF16)
+    w_out_ref[...] = w_out_full[...].astype(BF16)
+    w_degree_ref[...] = w_degree_full[...].astype(BF16)
+    w_species_ref[...] = w_species_full[...].astype(BF16)
     low = bessel.astype(BF16)
     bessel_ref[...] = low
-    weights = [w_in, w_hidden_ref[0].astype(BF16), w_hidden_ref[1].astype(BF16)]
+    weights = [w_in_ref[...], w_hidden_ref[0], w_hidden_ref[1]]
     for layer, weight in enumerate(weights):
         pre = dot_tn(weight, low)
         logistic = jax.nn.sigmoid(pre)
         low = (pre * logistic).astype(BF16)
         act_ref[layer] = low
         slope_ref[layer] = logistic * (1.0 + pre * (1.0 - logistic))
-    radial_ref[...] = dot_tn(w_out_ref[...].astype(BF16), low)
+    radial_ref[...] = dot_tn(w_out_ref[...], low)
 
     feats = feats_ref[...]
     kinds = w_species_ref.shape[0]
@@ -187,21 +243,17 @@
     total = jnp.zeros((channels, atoms), F32)
     for kind in range(kinds):
         masked = jnp.where(species_row == kind, feats.astype(F32), 0.0).astype(BF16)
-        total += dot_tn(w_species_ref[kind].astype(BF16), masked)
+        total += dot_tn(w_species_ref[kind], masked)
     self_ref[...] = total
 
     sources = live_sources(source_ref, count_ref)
+    source_ref[...] = sources
     for first in range(0, slots, TILE):
         hot = one_hot(index_row(sources, first, TILE), atoms)
         own_ref[:, first : first + TILE] = dot_nn(feats, hot).astype(BF16)
 
 
-def layer_kernel(
-    scale,
-    face_count,
-    count_ref,
-    *refs,
-):
+def layer_kernel(scale, face_count, *refs):
     face_in = refs[:face_count]
     (
         own_ref,
@@ -218,16 +270,17 @@
         target_ref,
         species_ref,
         cotangent_ref,
+        readout_ref,
         w_in_ref,
         w_hidden_ref,
         w_out_ref,
         w_degree_ref,
         w_species_ref,
-        readout_ref,
-    ) = refs[face_count : face_count + 20]
-    energy_ref, owned_ref, pack_ref = refs[face_count + 20 : face_count + 23]
-    face_out = refs[face_count + 23 : 2 * face_count + 23]
-    (
+        energy_ref,
+        pack_ref,
+        edge_back_ref,
+        back_local_ref,
+        target_hot_ref,
         weighted_ref,
         message_ref,
         summed_ref,
@@ -235,20 +288,16 @@
         mixed_back_ref,
         mixed_radial_ref,
         part_ref,
-        harm_back_ref,
         radial_back_ref,
-        stack_ref,
-        target_hot_ref,
-        source_hot_ref,
-    ) = refs[2 * face_count + 23 :]
+    ) = refs[face_count:]
     channels, atoms = feats_ref.shape
     slots = harm_ref.shape[1]
     kinds = w_species_ref.shape[0]
-    extended = source_hot_ref.shape[0]
+    borrow_count = 6 * LANES
     harm_count = harm_ref.shape[0]
-    w_degree = [w_degree_ref[d].astype(BF16) for d in range(4)]
-
-    sources = live_sources(source_ref, count_ref)
+    w_degree = [w_degree_ref[d] for d in range(4)]
+
+    sources = source_ref[...]
     targets = target_ref[...]
     pieces = []
     for ref in face_in:
@@ -257,11 +306,10 @@
     borrowed = jnp.concatenate(pieces, axis=1)
     for first in range(0, slots, TILE):
         cols = slice(first, first + TILE)
-        hot = one_hot(index_row(sources, first, TILE), extended)
-        source_hot_ref[:, cols] = hot
+        hot = one_hot(index_row(sources, first, TILE), borrow_count, atoms)
         target_hot_ref[:, cols] = one_hot(index_row(targets, first, TILE), atoms)
         weighted_ref[:, cols] = (
-            own_ref[:, cols].astype(F32) + dot_nn(borrowed, hot[atoms:, :])
+            own_ref[:, cols].astype(F32) + dot_nn(borrowed, hot)
         ) * scale
 
     for first in range(0, slots, TILE):
@@ -339,8 +387,9 @@
         mask = species_row == kind
         grad_species.append(dot_nt(jnp.where(mask, feats, 0.0).astype(BF16), back_self))
         back_local += dot_nn(
-            w_species_ref[kind].astype(BF16), jnp.where(mask, back_scalars, 0.0).astype(BF16)
+            w_species_ref[kind], jnp.where(mask, back_scalars, 0.0).astype(BF16)
         )
+    back_local_ref[...] = back_local
 
     for d in range(4):
         rows = slice(d * channels, (d + 1) * channels)
@@ -355,7 +404,7 @@
             for k in range(begin, end):
                 piece = gathered[k * channels : (k + 1) * channels, :]
                 part += piece * harm_ref[k : k + 1, cols]
-                harm_back_ref[k : k + 1, cols] = jnp.sum(
+                edge_back_ref[channels + k : channels + k + 1, cols] = jnp.sum(
                     piece * mixed_radial, axis=0, keepdims=True
                 )
             part_ref[d * channels : (d + 1) * channels, cols] = part
@@ -366,24 +415,73 @@
         mixed_part = dot_nn(w_degree[d], high) + dot_nn(w_degree[d], rest)
         radial_back_ref[rows, :] = (mixed_part * weighted_ref[...]).astype(BF16)
         back_weighted += mixed_part * radial_ref[rows, :]
-    back_weighted = back_weighted * scale
-    high, rest = halves(back_weighted)
+    edge_back_ref[0:channels, :] = back_weighted * scale
+
+    radial_back = radial_back_ref[...]
+    grad_out = dot_nt(act_ref[2], radial_back)
+    back_pre = (dot_nn(w_out_ref[...], radial_back) * slope_ref[2]).astype(BF16)
+    grad_hidden_two = dot_nt(act_ref[1], back_pre)
+    back_pre = (dot_nn(w_hidden_ref[1], back_pre) * slope_ref[1]).astype(BF16)
+    grad_hidden_one = dot_nt(act_ref[0], back_pre)
+    back_pre = (dot_nn(w_hidden_ref[0], back_pre) * slope_ref[0]).astype(BF16)
+    grad_in = dot_nt(bessel_ref[...], back_pre)
+    back_bessel = dot_nn(w_in_ref[...], back_pre)
+    edge_back_ref[channels : channels + 1, :] = jnp.sum(
+        back_bessel * slope_b_ref[...], axis=0, keepdims=True
+    )
+    edge_back_ref[channels + harm_count : channels + harm_count + 4, :] = geo_ref[...]
+
+    def packed(pair):
+        return jnp.concatenate(pair, axis=1).astype(pack_ref.dtype)
+
+    pack_ref[0:64, :] = grad_out[:, :LANES].astype(pack_ref.dtype)
+    pack_ref[64:128, :] = grad_out[:, LANES:].astype(pack_ref.dtype)
+    pack_ref[128:192, :] = packed([grad_degree[0], grad_degree[1]])
+    pack_ref[192:256, :] = packed([grad_degree[2], grad_degree[3]])
+    pack_ref[256:320, :] = packed([grad_species[0], grad_species[1]])
+    pack_ref[320:384, :] = packed([grad_species[2], grad_species[3]])
+    pack_ref[384:448, :] = packed([grad_hidden_one, grad_hidden_two])
+    pack_ref[448:456, :] = packed([grad_in, grad_readout])
+    if pack_ref.shape[0] > PACK_ROWS:
+        pack_ref[PACK_ROWS:, :] = jnp.zeros((pack_ref.shape[0] - PACK_ROWS, LANES), pack_ref.dtype)
+
+
+def spread_kernel(
+    count_ref,
+    edge_back_in,
+    back_local_in,
+    source_in,
+    target_in,
+    owned_ref,
+    *refs,
+):
+    face_out, refs = refs[:-6], refs[-6:]
+    edge_back_ref, back_local_ref, source_ref, target_ref, stack_ref, sems = refs
+    copies = fetch(
+        [
+            (source_in, source_ref),
+            (target_in, target_ref),
+            (edge_back_in, edge_back_ref),
+            (back_local_in, back_local_ref),
+        ],
+        sems,
+    )
+    channels, atoms = back_local_ref.shape
+    slots = edge_back_ref.shape[1]
+    harm_count = 16
+    for copy in copies:
+        copy.wait()
+    sources = live_sources(source_ref, count_ref)
+    targets = target_ref[...]
+    high, rest = halves(edge_back_ref[0:channels, :])
     stack_ref[0:channels, :] = high
     stack_ref[BACK_ROWS : BACK_ROWS + channels, :] = rest
-
-    radial_back = radial_back_ref[...]
-    grad_out = dot_nt(act_ref[2], radial_back)
-    back_pre = (dot_nn(w_out_ref[...].astype(BF16), radial_back) * slope_ref[2]).astype(BF16)
-    grad_hidden_two = dot_nt(act_ref[1], back_pre)
-    back_pre = (dot_nn(w_hidden_ref[1].astype(BF16), back_pre) * slope_ref[1]).astype(BF16)
-    grad_hidden_one = dot_nt(act_ref[0], back_pre)
-    back_pre = (dot_nn(w_hidden_ref[0].astype(BF16), back_pre) * slope_ref[0]).astype(BF16)
-    grad_in = dot_nt(bessel_ref[...], back_pre)
-    back_bessel = dot_nn(w_in_ref[...].astype(BF16), back_pre)
-
-    back_dist = jnp.sum(back_bessel * slope_b_ref[...], axis=0, keepdims=True)
-    x, y, z, inverse = (geo_ref[n : n + 1, :] for n in range(4))
-    g = [None] + [harm_back_ref[k : k + 1, :] for k in range(1, harm_count)]
+    back_dist = edge_back_ref[channels : channels + 1, :]
+    x, y, z, inverse = (
+        edge_back_ref[channels + harm_count + n : channels + harm_count + n + 1, :]
+        for n in range(4)
+    )
+    g = [edge_back_ref[channels + k : channels + k + 1, :] for k in range(harm_count)]
     xx, yy, zz = x * x, y * y, z * z
     five = CUBIC_C * (5.0 * zz - 1.0)
     three = 3.0 * CUBIC_A * (xx - yy)
@@ -425,12 +523,18 @@
     high, rest = halves(back_relative)
     stack_ref[channels:BACK_ROWS, :] = high
     stack_ref[BACK_ROWS + channels :, :] = rest
-    spread = dot_nt(stack_ref[...], source_hot_ref[...])
+    both = jnp.concatenate([high, rest], axis=0)
+    spread, target_back = 0.0, 0.0
+    for first in range(0, slots, TILE):
+        cols = slice(first, first + TILE)
+        hot = one_hot(index_row(sources, first, TILE), atoms + 6 * LANES)
+        spread += dot_nt(stack_ref[:, cols], hot)
+        hot = one_hot(index_row(targets, first, TILE), atoms)
+        target_back += dot_nt(both[:, cols], hot)
     spread = spread[:BACK_ROWS, :] + spread[BACK_ROWS:, :]
-    target_back = dot_nt(jnp.concatenate([high, rest], axis=0), target_hot_ref[...])
     size = BACK_ROWS - channels
     target_back = target_back[:size, :] + target_back[size:, :]
-    owned_ref[0:channels, :] = spread[:channels, :atoms] + back_local
+    owned_ref[0:channels, :] = spread[:channels, :atoms] + back_local_ref[...]
     owned_ref[channels:, :] = spread[channels:, :atoms] - target_back
     face = 0
     for ref in face_out:
@@ -439,28 +543,24 @@
             ref[part * BACK_ROWS : (part + 1) * BACK_ROWS, :] = spread[:, start : start + LANES]
             face += 1
 
-    pack_ref[0:64, :] = grad_out[:, :LANES]
-    pack_ref[64:128, :] = grad_out[:, LANES:]
-    pack_ref[128:192, :] = jnp.concatenate([grad_degree[0], grad_degree[1]], axis=1)
-    pack_ref[192:256, :] = jnp.concatenate([grad_degree[2], grad_degree[3]], axis=1)
-    pack_ref[256:320, :] = jnp.concatenate([grad_species[0], grad_species[1]], axis=1)
-    pack_ref[320:384, :] = jnp.concatenate([grad_species[2], grad_species[3]], axis=1)
-    pack_ref[384:448, :] = jnp.concatenate([grad_hidden_one, grad_hidden_two], axis=1)
-    pack_ref[448:456, :] = jnp.concatenate([grad_in, grad_readout], axis=1)
-    if pack_ref.shape[0] > PACK_ROWS:
-        pack_ref[PACK_ROWS:, :] = jnp.zeros((pack_ref.shape[0] - PACK_ROWS, LANES), F32)
-
-
-def collect_kernel(face_count, parts_ref, owned_ref, halo_ref, *refs):
-    face_in = refs[:face_count]
-    share_ref, feature_ref, position_ref = refs[face_count:]
-    channels, atoms = feature_ref.shape
+
+def total_kernel(parts_ref, after_ref, share_ref):
     devices = parts_ref.shape[0]
     total = parts_ref[0].astype(F32)
     for n in range(1, devices):
         total += parts_ref[n].astype(F32)
     for n in range(devices):
         share_ref[n] = total
+
+
+def collect_kernel(owned_in, halo_in, *refs):
+    state_in, face_in, state_out = refs[:18], refs[18:-23], refs[-21:-3]
+    feature_ref, position_ref = refs[-23:-21]
+    owned_ref, halo_ref, sems = refs[-3:]
+    pairs = [(halo_in, halo_ref), (owned_in, owned_ref)] + list(zip(state_in, state_out))
+    for copy in fetch(pairs, sems):
+        copy.wait()
+    channels, atoms = feature_ref.shape
     pieces = []
     for ref in face_in:
         for part in range(ref.shape[0] // BACK_ROWS):
@@ -511,6 +611,10 @@
     count = lax.axis_size(axis)
     pairs = [(source, (source + steps) % count) for source in range(count)]
     return lax.ppermute(value, axis, pairs)
+
+
+def in_hbm(arrays):
+    return [pltpu.with_memory_space_constraint(array, pltpu.HBM) for array in arrays]
 
 
 def vmem(count):
@@ -537,13 +641,13 @@
     channels, atoms = node_feats.shape
     slots = edge_vectors.shape[1]
     width = halo_index.shape[1]
-    extended = atoms + 6 * width
     devices = lax.axis_size(AXES)
     scale = 1.0 / max(1, 5 * slots // (8 * atoms))
     share = -(-PACK_ROWS // devices)
     share = -(-share // 8) * 8
     params = pltpu.CompilerParams(vmem_limit_bytes=VMEM_LIMIT)
     smem = [pl.BlockSpec(memory_space=pltpu.SMEM)]
+    hbm = pl.BlockSpec(memory_space=pltpu.HBM)
 
     routes = []
     for axis in AXES:
@@ -558,17 +662,23 @@
     species = atom_species.reshape(atoms // LANES, LANES)
     cotangent = site_cotangent.reshape(atoms // LANES, LANES)
 
-    faces = pl.pallas_call(
+    feats, *faces = pl.pallas_call(
         pick_faces_kernel,
-        out_shape=[shape((parts * channels, width), BF16) for _, _, parts in routes],
-        in_specs=vmem(2),
-        out_specs=vmem(len(routes)),
+        out_shape=[shape((channels, atoms), BF16)]
+        + [shape((parts * channels, width), BF16) for _, _, parts in routes],
+        in_specs=[hbm] * 2,
+        out_specs=vmem(1 + len(routes)),
+        scratch_shapes=[
+            pltpu.VMEM(halo_index.shape, jnp.int32),
+            pltpu.SemaphoreType.DMA((2,)),
+        ],
         compiler_params=params,
         name="pick_faces",
-    )(node_feats, halo_index)
+    )(*in_hbm((node_feats, halo_index)))
     arrived = [shifted(face, axis, way) for face, (axis, way, _) in zip(faces, routes)]
 
-    edge_parts = pl.pallas_call(
+    sized = (radial_input, radial_hidden, radial_output, degree_mix, species_mix)
+    own, harm, geo, slope_b, *rest = pl.pallas_call(
         radial_kernel,
         out_shape=[
             shape((channels, slots), BF16),
@@ -580,9 +690,18 @@
             shape((3, channels, slots)),
             shape((4 * channels, slots)),
             shape((channels, atoms)),
-        ],
-        in_specs=smem + vmem(8),
-        out_specs=vmem(9),
+            shape(source.shape, jnp.int32),
+            shape(target.shape, jnp.int32),
+            shape(species.shape, jnp.int32),
+            shape(cotangent.shape),
+            shape(readout_weights.shape),
+        ]
+        + [shape(member.shape, BF16) for member in sized],
+        in_specs=smem + vmem(1) + [hbm] * 11,
+        out_specs=vmem(19),
+        scratch_shapes=[pltpu.VMEM(edge_vectors.shape, F32)]
+        + [pltpu.VMEM(member.shape, F32) for member in sized]
+        + [pltpu.SemaphoreType.DMA((11,))],
         compiler_params=params,
         name="radial",
         cost_estimate=pl.CostEstimate(
@@ -590,27 +709,25 @@
         ),
     )(
         edge_count,
-        node_feats,
-        edge_vectors,
-        source,
-        species,
-        radial_input,
-        radial_hidden,
-        radial_output,
-        species_mix,
-    )
-
-    results = pl.pallas_call(
+        feats,
+        *in_hbm(
+            (edge_vectors, source, target, species, cotangent) + sized + (readout_weights,)
+        ),
+    )
+
+    state = masters + moments + squares
+    energy, packed, edge_back, back_local = pl.pallas_call(
         lambda *refs: layer_kernel(scale, len(routes), *refs),
         out_shape=[
             shape((1, atoms)),
-            shape((BACK_ROWS, atoms)),
             shape((share * devices, LANES)),
-        ]
-        + [shape((parts * BACK_ROWS, width)) for _, _, parts in routes],
-        in_specs=smem + vmem(len(routes) + 20),
-        out_specs=vmem(3 + len(routes)),
+            pltpu.HBM((channels + 24, slots), F32),
+            pltpu.HBM((channels, atoms), F32),
+        ],
+        in_specs=vmem(len(routes) + 20),
+        out_specs=vmem(4),
         scratch_shapes=[
+            pltpu.VMEM((atoms, slots), BF16),
             pltpu.VMEM((channels, slots), F32),
             pltpu.VMEM((16 * channels, 2 * TILE), BF16),
             pltpu.VMEM((16 * channels, atoms), F32),
@@ -618,48 +735,62 @@
             pltpu.VMEM((16 * channels, atoms), BF16),
             pltpu.VMEM((4 * channels, slots), F32),
             pltpu.VMEM((4 * channels, slots), F32),
-            pltpu.VMEM((16, slots), F32),
             pltpu.VMEM((4 * channels, slots), BF16),
-            pltpu.VMEM((2 * BACK_ROWS, slots), BF16),
-            pltpu.VMEM((atoms, slots), BF16),
-            pltpu.VMEM((extended, slots), BF16),
         ],
         compiler_params=params,
         name="layer",
-    )(
-        edge_count,
-        *arrived,
-        *edge_parts,
-        node_feats,
-        source,
-        target,
-        species,
-        cotangent,
-        radial_input,
-        radial_hidden,
-        radial_output,
-        degree_mix,
-        species_mix,
-        readout_weights,
-    )
-    energy, owned, packed = results[:3]
-    returned = [
-        shifted(back, axis, -way) for back, (axis, way, _) in zip(results[3:], routes)
-    ]
+    )(*arrived, own, harm, geo, slope_b, *rest[:5], feats, *rest[5:])
     parts = lax.all_to_all(packed.reshape(devices, share, LANES), AXES, 0, 0, tiled=True)
-    shares, feature_grad, position_grad = pl.pallas_call(
-        lambda *refs: collect_kernel(len(routes), *refs),
-        out_shape=[
-            shape((devices, share, LANES)),
-            shape((channels, atoms)),
-            shape((3, atoms)),
-        ],
-        in_specs=vmem(3 + len(routes)),
-        out_specs=vmem(3),
+    owned, *returns = pl.pallas_call(
+        spread_kernel,
+        out_shape=[pltpu.HBM((BACK_ROWS, atoms), F32)]
+        + [pltpu.HBM((parts * BACK_ROWS, width), F32) for _, _, parts in routes],
+        in_specs=smem + [hbm] * 4,
+        out_specs=vmem(1 + len(routes)),
+        scratch_shapes=[
+            pltpu.VMEM((channels + 24, slots), F32),
+            pltpu.VMEM((channels, atoms), F32),
+            pltpu.VMEM(source.shape, jnp.int32),
+            pltpu.VMEM(target.shape, jnp.int32),
+            pltpu.VMEM((2 * BACK_ROWS, slots), BF16),
+            pltpu.SemaphoreType.DMA((4,)),
+        ],
+        compiler_params=params,
+        name="spread",
+        cost_estimate=pl.CostEstimate(
+            flops=2 * slots * 160 * 2048, bytes_accessed=8 << 20, transcendentals=0
+        ),
+    )(edge_count, *in_hbm((edge_back, back_local, source, target)))
+    returned = [shifted(back, axis, -way) for back, (axis, way, _) in zip(returns, routes)]
+    shares = pl.pallas_call(
+        total_kernel,
+        out_shape=shape((devices, share, LANES)),
+        in_specs=vmem(1) + [hbm],
+        out_specs=vmem(1)[0],
+        compiler_params=params,
+        name="total",
+        cost_estimate=pl.CostEstimate(
+            flops=1 << 33, bytes_accessed=8 << 20, transcendentals=0
+        ),
+    )(parts, *in_hbm((owned,)))
+    gradient = lax.all_to_all(shares, AXES, 0, 0, tiled=True).reshape(devices * share, LANES)
+    feature_grad, position_grad, *state = pl.pallas_call(
+        collect_kernel,
+        out_shape=[shape((channels, atoms)), shape((3, atoms))]
+        + [shape(member.shape) for member in state],
+        in_specs=[hbm] * 20 + vmem(len(routes)),
+        out_specs=vmem(20),
+        scratch_shapes=[
+            pltpu.VMEM((BACK_ROWS, atoms), F32),
+            pltpu.VMEM(halo_index.shape, jnp.int32),
+            pltpu.SemaphoreType.DMA((20,)),
+        ],
         compiler_params=params,
         name="collect",
-    )(parts, owned, halo_index, *returned)
-    gradient = lax.all_to_all(shares, AXES, 0, 0, tiled=True).reshape(devices * share, LANES)
+        cost_estimate=pl.CostEstimate(
+            flops=1 << 36, bytes_accessed=1 << 20, transcendentals=0
+        ),
+    )(*in_hbm((owned, halo_index) + state), *returned)
     updated = pl.pallas_call(
         update_kernel,
         out_shape=[shape(member.shape) for member in masters + masters + masters],
@@ -667,7 +798,7 @@
         out_specs=vmem(18),
         compiler_params=params,
         name="update",
-    )(gradient, *masters, *moments, *squares)
+    )(gradient, *state)
     return (energy.reshape(atoms), feature_grad, position_grad, *updated)
 
 

time: 75.8 us -> 56.7 us (0.75)
  local copies, waits for them, and re-layouts: 15.8 us -> 0 us
  blocking collectives: 12 us -> 0 us
  starting transfers between devices: 17.8 us -> 22.7 us
  Pallas kernels: 21.7 us -> 24.5 us
  waiting for transfers between devices: 5.83 us -> 7.4 us
    unnamed x78 -> x0, local copies, waits for them, and re-layouts: 15.8 us -> none
    all_to_all x1 -> x0, blocking collectives: 12 us -> none  [on_device(): lax.all_to_all(shares, AXES, 0, 0, tiled=True)]
    pallas_call x2 -> x4, Pallas kernels: 1.34 us -> 8.93 us  [the longest x1 4.27 us: on_device(): pl.pallas_call(spread_kernel, out_shape=[pltpu.HBM((BACK_ROWS, atoms), F3...]
    all_to_all x0 -> x1, waiting for transfers between devices: none -> 7.37 us  [on_device(): lax.all_to_all(shares, AXES, 0, 0, tiled=True)]
    ppermute x10, waiting for transfers between devices: 5.83 us -> 0.03 us  [shifted(): return lax.ppermute(value, axis, pairs)]
    pallas_call x1, Pallas kernels: 16.3 us -> 11.4 us  [on_device(): pl.pallas_call(lambda *refs: layer_kernel(scale, len(routes), *refs), out...]
    all_to_all x0 -> x1, starting transfers between devices: none -> 4.51 us  [on_device(): lax.all_to_all(shares, AXES, 0, 0, tiled=True)]
  transfers between devices with their start and end apart: 11 -> 12, of which waited for: 3 -> 1; matrix products, arithmetic and copies ran while one was open for 0% -> 0% of each run, Pallas kernels for 4% -> 19%
where the time goes in v2:
time: 56.7 us; the launch traced here: 56.3 us
  Pallas kernels  24.5 us (43%)
  starting transfers between devices  22.7 us (40%)
  waiting for transfers between devices  7.4 us (13%)
  between operations  1.6 us (3%)
    ppermute x10, starting transfers between devices, shifted(): return lax.ppermute(value, axis, pairs)  14.8 us
    pallas_call x1, Pallas kernels, on_device(): pl.pallas_call(lambda *refs: layer_kernel(scale, len(routes), *refs), out...  11.4 us
    all_to_all x1, waiting for transfers between devices, on_device(): lax.all_to_all(shares, AXES, 0, 0, tiled=True)  7.37 us
    all_to_all x1, starting transfers between devices, on_device(): lax.all_to_all(shares, AXES, 0, 0, tiled=True)  4.51 us
    pallas_call x1, Pallas kernels, on_device(): pl.pallas_call(spread_kernel, out_shape=[pltpu.HBM((BACK_ROWS, atoms), F3...  4.27 us
    all_to_all x1, starting transfers between devices, on_device(): lax.all_to_all(packed.reshape(devices, share, LANES), AXES, 0, 0, tiled=T...  3.38 us
    pallas_call x1, Pallas kernels, on_device(): pl.pallas_call(radial_kernel, out_shape=[shape((channels, slots), BF16),...  2.93 us
    pallas_call x1, Pallas kernels, on_device(): pl.pallas_call(collect_kernel, out_shape=[shape((channels, atoms)), shape...  2.8 us
  transfers between devices with their start and end apart: 12, of which 1 were waited for; matrix products, arithmetic and copies ran while one was open for 0% of the time, Pallas kernels for 19%

profile of v2, /device:TPU:0, one launch (start us, length us, event | category | flops | bytes accessed | tf_op | source)
XLA Modules:
  0.0 56.3 jit_solution(12334703675643479634)
XLA Ops:
  0.7 1.1 %pick_faces.1 = (bf16[64,512]{1,0:T(8,128)(2,1)S(1)}, bf16[128,128]{1,0:T(8,128)(2,1)S(1)}, bf16[64,128]{1,0:T(8,128)(2,1)S(1)}, bf16[64,128]{1,0:T(8,128)(2,1)S...) custom-call(bf16[64,512]{1,0:T(8,128)(2,1)} %feats_in.1, s32[6,128]{1,0:T(8,128)} %halo_in.3), custom_call_target="tpu_custom_call" | custom-call | tf_op jit(solution)/shard_map/pick_faces/pallas_call | solution.py:665
  1.8 3.0 %collective-permute-start = (bf16[128,128]{1,0:T(8,128)(2,1)S(1)}, bf16[128,128]{1,0:T(8,128)(2,1)S(1)}, u32[]{:S(2)}, u32[]{:S(2)}) collective-permute-start(bf16[128,128]{1,0:T(8,128)(2,1)S(1)} %get-tuple-element.94), channel_id=1, source_target_pairs={{0,16},{16,0},{1,17},{17,1},{2,18},{18,2},{3,19},{19,3},{4,20},{20... | collective-permute-start | bytes 98312 | tf_op jit(solution)/shard_map/ppermute | solution.py:613
  4.8 0.0 collective-permute-start.1
  4.8 1.7 %collective-permute-start.2 = (bf16[64,128]{1,0:T(8,128)(2,1)S(1)}, bf16[64,128]{1,0:T(8,128)(2,1)S(1)}, u32[]{:S(2)}, u32[]{:S(2)}) collective-permute-start(bf16[64,128]{1,0:T(8,128)(2,1)S(1)} %get-tuple-element.96), channel_id=1, source_target_pairs={{0,12},{4,0},{8,4},{12,8},{1,13},{5,1},{9,5},{13,9},{2,14},{6,2},{... | collective-permute-start | bytes 49160 | tf_op jit(solution)/shard_map/ppermute | solution.py:613
  6.5 1.6 %collective-permute-start.3 = (bf16[64,128]{1,0:T(8,128)(2,1)S(1)}, bf16[64,128]{1,0:T(8,128)(2,1)S(1)}, u32[]{:S(2)}, u32[]{:S(2)}) collective-permute-start(bf16[64,128]{1,0:T(8,128)(2,1)S(1)} %get-tuple-element.97), channel_id=1, source_target_pairs={{0,1},{1,2},{2,3},{3,0},{4,5},{5,6},{6,7},{7,4},{8,9},{9,10},{10,1... | collective-permute-start | bytes 49160 | tf_op jit(solution)/shard_map/ppermute | solution.py:613
  8.1 2.2 %collective-permute-start.4 = (bf16[64,128]{1,0:T(8,128)(2,1)S(1)}, bf16[64,128]{1,0:T(8,128)(2,1)S(1)}, u32[]{:S(2)}, u32[]{:S(2)}) collective-permute-start(bf16[64,128]{1,0:T(8,128)(2,1)S(1)} %get-tuple-element.98), channel_id=1, source_target_pairs={{0,3},{1,0},{2,1},{3,2},{4,7},{5,4},{6,5},{7,6},{8,11},{9,8},{10,9... | collective-permute-start | bytes 49160 | tf_op jit(solution)/shard_map/ppermute | solution.py:613
  11.0 2.9 %radial.1 = (bf16[64,2048]{1,0:T(8,128)(2,1)S(1)}, f32[16,2048]{1,0:T(8,128)S(1)}, f32[4,2048]{1,0:T(4,128)S(1)}, f32[8,2048]{1,0:T(8,128)S(1)}, bf16[8,2048]{1,...) custom-call(s32[1]{0:T(128)S(6)} %copy.47.count_ref, ...), custom_call_target="tpu_custom_call" | custom-call | flops 268435456 | bytes 8388608 | tf_op jit(solution)/shard_map/radial/pallas_call | solution.py:681
  14.0 0.0 collective-permute-done.1.refs_1_
  14.0 0.0 collective-permute-done.2.refs_2_
  14.0 0.0 collective-permute-done.3.refs_3_
  14.0 0.0 collective-permute-done.4.refs_4_
  14.0 0.0 collective-permute-done.refs_0_
  14.0 11.4 %layer.1 = (f32[1,512]{1,0:T(1,128)}, f32[512,128]{1,0:T(8,128)}, f32[88,2048]{1,0:T(8,128)}, f32[64,512]{1,0:T(8,128)}) custom-call(bf16[128,128]{1,0:T(8,128)(2,1)S(1)} %collective-permute-done.refs_0_, bf16[64,128]{1,0:T(8,128)(2,1)S(1)} %collective-permute-done.1.refs_1_, bf16[64,128]{1,0:T(8,128)(2,1)S(1)} %collective-permute-done.2.refs_2_, ...), custom_call_target="tpu_custom_call" | custom-call | tf_op jit(solution)/shard_map/layer/pallas_call | solution.py:719
  25.4 3.4 %all-to-all-start = ((f32[32,16,128]{2,1,0:T(8,128)}), f32[32,16,128]{2,1,0:T(8,128)S(1)}, u32[]{:S(2)}, u32[]{:S(2)}) async-start(f32[32,16,128]{2,1,0:T(8,128)} %bitcast.5), calls=%async_computation | async-start | bytes 524288 | tf_op jit(solution)/shard_map/all_to_all | solution.py:743
  28.8 4.3 %spread.1 = (f32[80,512]{1,0:T(8,128)}, f32[160,128]{1,0:T(8,128)}, f32[80,128]{1,0:T(8,128)}, f32[80,128]{1,0:T(8,128)}, f32[80,128]{1,0:T(8,128)}, /*index=5*/f32[80,128]{1,0:T(8,128)}) custom-call(s32[1]{0:T(128)S(6)} %copy.47.count_ref, f32[88,2048]{1,0:T(8,128)} %get-tuple-element.120.edge_back_in, f32[64,512]{1,0:T(8,128)} %get-tuple-element.121.back_local_in, ...), custom_call_target="tpu_custom_call" | custom-call | flops 1342177280 | bytes 8388608 | tf_op jit(solution)/shard_map/spread/pallas_call | solution.py:744
  33.1 1.4 %collective-permute-start.6 = (f32[80,128]{1,0:T(8,128)}, f32[80,128]{1,0:T(8,128)S(1)}, u32[]{:S(2)}, u32[]{:S(2)}) collective-permute-start(f32[80,128]{1,0:T(8,128)} %get-tuple-element.124), channel_id=1, source_target_pairs={{0,12},{4,0},{8,4},{12,8},{1,13},{5,1},{9,5},{13,9},{2,14},{6,2},{... | collective-permute-start | bytes 122888 | tf_op jit(solution)/shard_map/ppermute | solution.py:613
  34.5 0.0 collective-permute-start.7
  34.5 3.3 %collective-permute-start.8 = (f32[80,128]{1,0:T(8,128)}, f32[80,128]{1,0:T(8,128)S(1)}, u32[]{:S(2)}, u32[]{:S(2)}) collective-permute-start(f32[80,128]{1,0:T(8,128)} %get-tuple-element.126), channel_id=1, source_target_pairs={{0,3},{1,0},{2,1},{3,2},{4,7},{5,4},{6,5},{7,6},{8,11},{9,8},{10,9... | collective-permute-start | bytes 122888 | tf_op jit(solution)/shard_map/ppermute | solution.py:613
  37.8 0.0 collective-permute-start.9
  37.8 1.5 %collective-permute-start.5 = (f32[160,128]{1,0:T(8,128)}, f32[160,128]{1,0:T(8,128)S(1)}, u32[]{:S(2)}, u32[]{:S(2)}) collective-permute-start(f32[160,128]{1,0:T(8,128)} %get-tuple-element.123), channel_id=1, source_target_pairs={{0,16},{16,0},{1,17},{17,1},{2,18},{18,2},{3,19},{19,3},{4,20},{20... | collective-permute-start | bytes 245768 | tf_op jit(solution)/shard_map/ppermute | solution.py:613
  39.3 0.0 all-to-all-done.parts_ref
  39.3 0.7 %total.1 = f32[32,16,128]{2,1,0:T(8,128)} custom-call(f32[32,16,128]{2,1,0:T(8,128)S(1)} %all-to-all-done.parts_ref, f32[80,512]{1,0:T(8,128)} %get-tuple-element.122.owned_in.after_ref), custom_call_target="tpu_custom_call" | custom-call | flops 8589934592 | bytes 8388608 | tf_op jit(solution)/shard_map/total/pallas_call | solution.py:765
  40.1 4.5 %all-to-all-start.1 = ((f32[32,16,128]{2,1,0:T(8,128)}), f32[32,16,128]{2,1,0:T(8,128)S(1)}, u32[]{:S(2)}, u32[]{:S(2)}) async-start(f32[32,16,128]{2,1,0:T(8,128)} %total.1), calls=%async_computation.1 | async-start | bytes 524288 | tf_op jit(solution)/shard_map/all_to_all | solution.py:776
  44.6 0.0 collective-permute-done.6.refs_19_
  44.6 0.0 collective-permute-done.7.refs_20_
  44.6 0.0 collective-permute-done.8.refs_21_
  44.6 0.0 collective-permute-done.9.refs_22_
  44.6 0.0 collective-permute-done.5.refs_18_
  44.7 2.8 %collect.1 = (f32[64,512]{1,0:T(8,128)}, f32[3,512]{1,0:T(4,128)}, f32[8,64]{1,0:T(8,128)S(1)}, f32[2,64,64]{2,1,0:T(8,128)S(1)}, f32[64,256]{1,0:T(8,128)S(1)},...) custom-call(f32[80,512]{1,0:T(8,128)} %get-tuple-element.122.owned_i, ...), custom_call_target="tpu_custom_call" | custom-call | flops 68719476736 | bytes 1048576 | tf_op jit(solution)/shard_map/collect/pallas_call | solution.py:777
  47.5 7.4 %all-to-all-done.1 = f32[32,16,128]{2,1,0:T(8,128)S(1)} async-done(((f32[32,16,128]{2,1,0:T(8,128)}), f32[32,16,128]{2,1,0:T(8,128)S(1)}, u32[]{:S(2)}, u32[]{:S(2)}) %all-to-all-start.1) | async-done | bytes 262176 | tf_op jit(solution)/shard_map/all_to_all | solution.py:776
  54.8 1.3 %update.1 = (f32[8,64]{1,0:T(8,128)}, f32[2,64,64]{2,1,0:T(8,128)}, f32[64,256]{1,0:T(8,128)}, f32[4,64,64]{2,1,0:T(8,128)}, f32[4,64,64]{2,1,0:T(8,128)}, /*ind...) custom-call(f32[512,128]{1,0:T(8,128)S(1)} %bitcast.7, ...), custom_call_target="tpu_custom_call" | custom-call | tf_op jit(solution)/shard_map/update/pallas_call | solution.py:794
Async XLA Ops:
  1.8 12.2 %collective-permute-start = (bf16[128,128]{1,0:T(8,128)(2,1)S(1)}, bf16[128,128]{1,0:T(8,128)(2,1)S(1)}, u32[]{:S(2)}, u32[]{:S(2)}) collective-permute-start(bf16[128,128]{1,0:T(8,128)(2,1)S(1)} %get-tuple-element.94), channel_id=1, source_target_pairs={{0,16},{16,0},{1,17},{17,1},{2,18},{18,2},{3,19},{19,3},{4,20},{20... | collective-permute-start | bytes 98312 | tf_op jit(solution)/shard_map/ppermute | solution.py:613
  4.8 9.2 %collective-permute-start.1 = (bf16[64,128]{1,0:T(8,128)(2,1)S(1)}, bf16[64,128]{1,0:T(8,128)(2,1)S(1)}, u32[]{:S(2)}, u32[]{:S(2)}) collective-permute-start(bf16[64,128]{1,0:T(8,128)(2,1)S(1)} %get-tuple-element.95), channel_id=1, source_target_pairs={{0,4},{4,8},{8,12},{12,0},{1,5},{5,9},{9,13},{13,1},{2,6},{6,10},{... | collective-permute-start | bytes 49160 | tf_op jit(solution)/shard_map/ppermute | solution.py:613
  4.8 9.2 %collective-permute-start.2 = (bf16[64,128]{1,0:T(8,128)(2,1)S(1)}, bf16[64,128]{1,0:T(8,128)(2,1)S(1)}, u32[]{:S(2)}, u32[]{:S(2)}) collective-permute-start(bf16[64,128]{1,0:T(8,128)(2,1)S(1)} %get-tuple-element.96), channel_id=1, source_target_pairs={{0,12},{4,0},{8,4},{12,8},{1,13},{5,1},{9,5},{13,9},{2,14},{6,2},{... | collective-permute-start | bytes 49160 | tf_op jit(solution)/shard_map/ppermute | solution.py:613
  6.5 7.4 %collective-permute-start.3 = (bf16[64,128]{1,0:T(8,128)(2,1)S(1)}, bf16[64,128]{1,0:T(8,128)(2,1)S(1)}, u32[]{:S(2)}, u32[]{:S(2)}) collective-permute-start(bf16[64,128]{1,0:T(8,128)(2,1)S(1)} %get-tuple-element.97), channel_id=1, source_target_pairs={{0,1},{1,2},{2,3},{3,0},{4,5},{5,6},{6,7},{7,4},{8,9},{9,10},{10,1... | collective-permute-start | bytes 49160 | tf_op jit(solution)/shard_map/ppermute | solution.py:613
  8.1 5.9 %collective-permute-start.4 = (bf16[64,128]{1,0:T(8,128)(2,1)S(1)}, bf16[64,128]{1,0:T(8,128)(2,1)S(1)}, u32[]{:S(2)}, u32[]{:S(2)}) collective-permute-start(bf16[64,128]{1,0:T(8,128)(2,1)S(1)} %get-tuple-element.98), channel_id=1, source_target_pairs={{0,3},{1,0},{2,1},{3,2},{4,7},{5,4},{6,5},{7,6},{8,11},{9,8},{10,9... | collective-permute-start | bytes 49160 | tf_op jit(solution)/shard_map/ppermute | solution.py:613
  25.4 13.9 %all-to-all-start = ((f32[32,16,128]{2,1,0:T(8,128)}), f32[32,16,128]{2,1,0:T(8,128)S(1)}, u32[]{:S(2)}, u32[]{:S(2)}) async-start(f32[32,16,128]{2,1,0:T(8,128)} %bitcast.5), calls=%async_computation | async-start | bytes 524288 | tf_op jit(solution)/shard_map/all_to_all | solution.py:743
  33.1 11.5 %collective-permute-start.6 = (f32[80,128]{1,0:T(8,128)}, f32[80,128]{1,0:T(8,128)S(1)}, u32[]{:S(2)}, u32[]{:S(2)}) collective-permute-start(f32[80,128]{1,0:T(8,128)} %get-tuple-element.124), channel_id=1, source_target_pairs={{0,12},{4,0},{8,4},{12,8},{1,13},{5,1},{9,5},{13,9},{2,14},{6,2},{... | collective-permute-start | bytes 122888 | tf_op jit(solution)/shard_map/ppermute | solution.py:613
  34.5 10.1 %collective-permute-start.7 = (f32[80,128]{1,0:T(8,128)}, f32[80,128]{1,0:T(8,128)S(1)}, u32[]{:S(2)}, u32[]{:S(2)}) collective-permute-start(f32[80,128]{1,0:T(8,128)} %get-tuple-element.125), channel_id=1, source_target_pairs={{0,4},{4,8},{8,12},{12,0},{1,5},{5,9},{9,13},{13,1},{2,6},{6,10},{... | collective-permute-start | bytes 122888 | tf_op jit(solution)/shard_map/ppermute | solution.py:613
  34.5 10.1 %collective-permute-start.8 = (f32[80,128]{1,0:T(8,128)}, f32[80,128]{1,0:T(8,128)S(1)}, u32[]{:S(2)}, u32[]{:S(2)}) collective-permute-start(f32[80,128]{1,0:T(8,128)} %get-tuple-element.126), channel_id=1, source_target_pairs={{0,3},{1,0},{2,1},{3,2},{4,7},{5,4},{6,5},{7,6},{8,11},{9,8},{10,9... | collective-permute-start | bytes 122888 | tf_op jit(solution)/shard_map/ppermute | solution.py:613
  37.8 6.8 %collective-permute-start.9 = (f32[80,128]{1,0:T(8,128)}, f32[80,128]{1,0:T(8,128)S(1)}, u32[]{:S(2)}, u32[]{:S(2)}) collective-permute-start(f32[80,128]{1,0:T(8,128)} %get-tuple-element.127), channel_id=1, source_target_pairs={{0,1},{1,2},{2,3},{3,0},{4,5},{5,6},{6,7},{7,4},{8,9},{9,10},{10,1... | collective-permute-start | bytes 122888 | tf_op jit(solution)/shard_map/ppermute | solution.py:613
  37.8 6.8 %collective-permute-start.5 = (f32[160,128]{1,0:T(8,128)}, f32[160,128]{1,0:T(8,128)S(1)}, u32[]{:S(2)}, u32[]{:S(2)}) collective-permute-start(f32[160,128]{1,0:T(8,128)} %get-tuple-element.123), channel_id=1, source_target_pairs={{0,16},{16,0},{1,17},{17,1},{2,18},{18,2},{3,19},{19,3},{4,20},{20... | collective-permute-start | bytes 245768 | tf_op jit(solution)/shard_map/ppermute | solution.py:613
  40.1 14.7 %all-to-all-start.1 = ((f32[32,16,128]{2,1,0:T(8,128)}), f32[32,16,128]{2,1,0:T(8,128)S(1)}, u32[]{:S(2)}, u32[]{:S(2)}) async-start(f32[32,16,128]{2,1,0:T(8,128)} %total.1), calls=%async_computation.1 | async-start | bytes 524288 | tf_op jit(solution)/shard_map/all_to_all | solution.py:776
